TPU v7x, 256 devices: a whole 4x4x8 slice. The times are simulated.
256 devices in a mesh: group: 8 (over z), member: 32 (over y, x, core).
Axes of the slice: x: 4, y: 4, z: 8, core: 2. Of those that a mesh axis runs over, the one named last changes fastest.
Arguments:
- embeddings: bfloat16 [196608, 1024], P(('group', 'member')), may hold values from -18 to 18
- prior: float32 [196608, 1000], P(('group', 'member')), may hold values from 0.05 to 5
- source_member: int32 [8, 32, 4], P('group'), may hold values from 0 to 31, as said below
- source_block: int32 [8, 32, 4], P('group'), may hold values from 0 to 5
- cross_block: int32 [8, 32, 2], P(None, 'member'), may hold values from 0 to 5
- row_links: int32 [196608, 4], P(('group', 'member')), may hold values from 0 to 5
Outputs:
- propagated: float32 [196608, 1000], P(('group', 'member'))
Inputs may be any that keep to these rules, and one draw needn't show every extreme that they name: `source_member`: no device names itself, and the members in one device's list are distinct. Over all lists of one group no member is named more than 7 times, and in every group some member is named exactly 7 times.
All inputs are finite; a program needn't handle non-finite values.
Results may differ from a plain program's by a relative error of at most 0.0079.
Values may be sent and summed in bfloat16 or wider, within the bound.
No kernel may reach another device: no remote copies, remote signals or barrier semaphores. Data moves between devices by JAX's collectives and lax.ppermute only.
A program may use at most 64 MiB of HBM per device.

v0:
```python
import jax
import jax.numpy as jnp
from jax import lax
from jax.experimental import pallas as pl
from jax.experimental.pallas import tpu as pltpu
from jax.sharding import PartitionSpec as P

BR = 128
MIXING = 0.8
SUB = 32
QB = 256
BF = jnp.bfloat16
F32 = jnp.float32
VMEM_BYTES = 24 * 1024 * 1024


def params():
    return pltpu.CompilerParams(
        dimension_semantics=("arbitrary",), vmem_limit_bytes=VMEM_BYTES
    )


def cost(flops, size, exps=0):
    return pl.CostEstimate(flops=flops, bytes_accessed=size, transcendentals=exps)


def nt(a, b):
    return lax.dot_general(a, b, (((1,), (1,)), ((), ())), preferred_element_type=F32)


def nn(a, b):
    return jnp.dot(a, b, preferred_element_type=F32)


def padded(x, rows):
    return jnp.concatenate([x, jnp.zeros((rows - x.shape[0], x.shape[1]), x.dtype)], axis=0)


def share_of(prior_ref):
    prior = prior_ref[...]
    return prior / jnp.sum(prior, axis=0, keepdims=True)


def prep_kernel(prior_ref, emb_ref, out_ref):
    relays = out_ref.shape[0]
    labels = padded(share_of(prior_ref), relays * SUB).astype(BF)
    out_ref[:, :SUB, :] = labels.reshape(relays, SUB, BR)
    wide = emb_ref.shape[1] // BR
    for r in range(BR // SUB):
        for f in range(wide):
            out_ref[r * wide + f, SUB:, :] = emb_ref[r * SUB : (r + 1) * SUB, f * BR : (f + 1) * BR]


def prep(prior_t, emb, relays):
    classes, rows = prior_t.shape
    features = emb.shape[1]
    return pl.pallas_call(
        prep_kernel,
        grid=(rows // BR,),
        in_specs=[
            pl.BlockSpec((classes, BR), lambda i: (0, i)),
            pl.BlockSpec((BR, features), lambda i: (i, 0)),
        ],
        out_specs=pl.BlockSpec((relays, 2 * SUB, BR), lambda i: (0, 0, i)),
        out_shape=jax.ShapeDtypeStruct((relays, 2 * SUB, rows), BF),
        compiler_params=params(),
        cost_estimate=cost(4 * classes * rows, 4 * classes * rows + 4 * features * rows),
        name="prep",
    )(prior_t, emb)


def select_kernel(owner_ref, block_ref, got_ref, out_ref):
    members, slots = owner_ref.shape

    @pl.loop(0, members)
    def _(d):
        for k in range(slots):
            lane = pl.multiple_of(block_ref[d, k] * BR, BR)
            out_ref[d, :, k * BR : (k + 1) * BR] = got_ref[owner_ref[d, k], :, pl.ds(lane, BR)]


def select(owners, blocks, got):
    members, slots = owners.shape
    depth = got.shape[1]
    return pl.pallas_call(
        select_kernel,
        in_specs=[
            pl.BlockSpec(memory_space=pltpu.SMEM),
            pl.BlockSpec(memory_space=pltpu.SMEM),
            pl.BlockSpec(memory_space=pltpu.VMEM),
        ],
        out_specs=pl.BlockSpec(memory_space=pltpu.VMEM),
        out_shape=jax.ShapeDtypeStruct((members, depth, slots * BR), BF),
        compiler_params=pltpu.CompilerParams(vmem_limit_bytes=VMEM_BYTES),
        cost_estimate=cost(0, 4 * got.size),
        name="select",
    )(owners, blocks, got)


def pack_kernel(pick_ref, emb_ref, lab_ref, out_ref):
    out_ref[:BR] = emb_ref[...]
    labels = lab_ref[...].reshape(-1, BR)
    for f in range(labels.shape[0] // BR):
        out_ref[BR:, f * BR : (f + 1) * BR] = labels[f * BR : (f + 1) * BR]


def pack(pick, emb, spread):
    relays = spread.shape[0]
    features = emb.shape[1]
    return pl.pallas_call(
        pack_kernel,
        grid_spec=pltpu.PrefetchScalarGridSpec(
            num_scalar_prefetch=1,
            grid=(1,),
            in_specs=[
                pl.BlockSpec((BR, features), lambda i, p: (p[0], 0)),
                pl.BlockSpec((relays, SUB, BR), lambda i, p: (0, 0, p[0])),
            ],
            out_specs=pl.BlockSpec((2 * BR, features), lambda i, p: (0, 0)),
        ),
        out_shape=jax.ShapeDtypeStruct((2 * BR, features), BF),
        compiler_params=params(),
        cost_estimate=cost(0, 8 * BR * features),
        name="pack_cross",
    )(pick, emb, spread)


def pack_labels_kernel(pick_ref, lab_ref, out_ref):
    out_ref[...] = lab_ref[...]


def pack_labels(pick, labels_t):
    depth = labels_t.shape[0]
    return pl.pallas_call(
        pack_labels_kernel,
        grid_spec=pltpu.PrefetchScalarGridSpec(
            num_scalar_prefetch=1,
            grid=(1,),
            in_specs=[pl.BlockSpec((depth, BR), lambda i, p: (0, p[0]))],
            out_specs=pl.BlockSpec((depth, BR), lambda i, p: (0, 0)),
        ),
        out_shape=jax.ShapeDtypeStruct((depth, BR), BF),
        compiler_params=params(),
        cost_estimate=cost(0, 4 * BR * depth),
        name="pack_labels",
    )(pick, labels_t)


def slot_hit(links, slot):
    return jnp.max(jnp.where(links == slot, 1.0, 0.0), axis=0, keepdims=True) > 0.0


def own_kernel(near_slots, emb_ref, q_ref, lab_ref, below_ref, above_ref, links_ref, p_ref, mix_ref, stat_ref, far_ref):
    step = pl.program_id(0)
    rows, features = emb_ref.shape
    depth = mix_ref.shape[0]

    @pl.when(step == 0)
    def _():
        for f in range(depth // BR):
            for s, ref in enumerate((below_ref, above_ref)):
                far_ref[f * BR : (f + 1) * BR, s * BR : (s + 1) * BR] = ref[BR:, f * BR : (f + 1) * BR]

    q = q_ref[...]
    scale = features ** (-0.5)
    own = nt(emb_ref[...], q) * scale
    key_id = lax.broadcasted_iota(jnp.int32, own.shape, 0)
    row_id = lax.broadcasted_iota(jnp.int32, own.shape, 1) + step * QB
    own = jnp.where(key_id == row_id, -jnp.inf, own)
    links = links_ref[...]
    parts = [own]
    for s, ref in enumerate((below_ref, above_ref)):
        far = nt(ref[:BR], q) * scale
        parts.append(jnp.where(slot_hit(links, near_slots + s), far, -jnp.inf))
    scores = jnp.concatenate(parts, axis=0)
    top = jnp.max(scores, axis=0, keepdims=True)
    powers = jnp.exp(scores - top)
    total = jnp.sum(powers, axis=0, keepdims=True)
    powers = powers.astype(BF)
    p_ref[...] = powers
    mix_ref[...] = nn(lab_ref[...].reshape(depth, rows), powers[:rows]) + nn(far_ref[...], powers[rows:])
    stat_ref[...] = jnp.concatenate([top, total, jnp.zeros((6, QB), F32)], axis=0)


def own_part(emb, spread, below, above, links_t, near_slots):
    rows, features = emb.shape
    relays = spread.shape[0]
    depth = relays * SUB
    keys = rows + 2 * BR
    return pl.pallas_call(
        lambda *refs: own_kernel(near_slots, *refs),
        grid=(rows // QB,),
        in_specs=[
            pl.BlockSpec((rows, features), lambda i: (0, 0)),
            pl.BlockSpec((QB, features), lambda i: (i, 0)),
            pl.BlockSpec((relays, SUB, rows), lambda i: (0, 0, 0)),
            pl.BlockSpec((2 * BR, features), lambda i: (0, 0)),
            pl.BlockSpec((2 * BR, features), lambda i: (0, 0)),
            pl.BlockSpec((links_t.shape[0], QB), lambda i: (0, i)),
        ],
        out_specs=[
            pl.BlockSpec((keys, QB), lambda i: (0, i)),
            pl.BlockSpec((depth, QB), lambda i: (0, i)),
            pl.BlockSpec((8, QB), lambda i: (0, i)),
        ],
        out_shape=[
            jax.ShapeDtypeStruct((keys, rows), BF),
            jax.ShapeDtypeStruct((depth, rows), F32),
            jax.ShapeDtypeStruct((8, rows), F32),
        ],
        scratch_shapes=[pltpu.VMEM((depth, 2 * BR), BF)],
        compiler_params=params(),
        cost_estimate=cost(4 * keys * rows * features, 12 * depth * rows, keys * rows),
        name="own_part",
    )(emb, emb, spread, below, above, links_t)


def near_kernel(got_ref, q_ref, links_ref, mix_ref, stat_ref, prior_ref, lab_ref, p_ref, out_ref, key_ref):
    step = pl.program_id(0)
    features = q_ref.shape[1]
    relays = got_ref.shape[0]
    slots = got_ref.shape[2] // BR
    wide = features // BR

    @pl.when(step == 0)
    def _():
        for s in range(slots):
            for r in range(BR // SUB):
                at = s * BR + r * SUB
                for f in range(wide):
                    key_ref[at : at + SUB, f * BR : (f + 1) * BR] = got_ref[
                        r * wide + f, SUB:, s * BR : (s + 1) * BR
                    ]

    links = links_ref[...]
    scores = nt(key_ref[...], q_ref[...]) * features ** (-0.5)
    scores = jnp.concatenate(
        [
            jnp.where(slot_hit(links, s), scores[s * BR : (s + 1) * BR], -jnp.inf)
            for s in range(slots)
        ],
        axis=0,
    )
    own_top = stat_ref[0:1]
    top = jnp.maximum(own_top, jnp.max(scores, axis=0, keepdims=True))
    powers = jnp.exp(scores - top)
    lower = jnp.exp(own_top - top)
    inverse = MIXING / (lower * stat_ref[1:2] + jnp.sum(powers, axis=0, keepdims=True))
    lower = lower * inverse
    powers = powers.astype(BF)
    p_ref[...] = powers
    out_ref[...] = jnp.concatenate([lower, inverse, jnp.zeros((6, QB), F32)], axis=0)
    near = nn(got_ref[:, :SUB, :].reshape(relays * SUB, slots * BR), powers)
    sharp = sharpened(mix_ref[...] * lower + near * inverse, prior_ref)
    lab_ref[...] = padded(sharp, relays * SUB).astype(BF)


def sharpened(mixed, prior_ref):
    share = share_of(prior_ref)
    mixed = mixed[: share.shape[0]] + (1.0 - MIXING) * share
    squared = mixed * mixed
    return squared / jnp.sum(squared, axis=0, keepdims=True)


def near_part(got, emb, links_t, mix, stat, prior_t):
    rows, features = emb.shape
    relays, depth2, near_keys = got.shape
    classes = prior_t.shape[0]
    depth = relays * SUB
    return pl.pallas_call(
        near_kernel,
        grid=(rows // QB,),
        in_specs=[
            pl.BlockSpec((relays, depth2, near_keys), lambda i: (0, 0, 0)),
            pl.BlockSpec((QB, features), lambda i: (i, 0)),
            pl.BlockSpec((links_t.shape[0], QB), lambda i: (0, i)),
            pl.BlockSpec((depth, QB), lambda i: (0, i)),
            pl.BlockSpec((8, QB), lambda i: (0, i)),
            pl.BlockSpec((classes, QB), lambda i: (0, i)),
        ],
        out_specs=[
            pl.BlockSpec((depth, QB), lambda i: (0, i)),
            pl.BlockSpec((near_keys, QB), lambda i: (0, i)),
            pl.BlockSpec((8, QB), lambda i: (0, i)),
        ],
        out_shape=[
            jax.ShapeDtypeStruct((depth, rows), BF),
            jax.ShapeDtypeStruct((near_keys, rows), BF),
            jax.ShapeDtypeStruct((8, rows), F32),
        ],
        scratch_shapes=[pltpu.VMEM((near_keys, features), BF)],
        compiler_params=params(),
        cost_estimate=cost(4 * near_keys * rows * features, 12 * depth * rows, near_keys * rows),
        name="near_part",
    )(got, emb, links_t, mix, stat, prior_t)


def remix_kernel(lab_ref, below_ref, above_ref, p_ref, out_ref):
    rows = lab_ref.shape[1]
    far = jnp.concatenate([below_ref[...], above_ref[...]], axis=1)
    out_ref[...] = nn(lab_ref[...], p_ref[:rows]) + nn(far, p_ref[rows:])


def remix(labels_t, below, above, powers):
    depth, rows = labels_t.shape
    keys = powers.shape[0]
    return pl.pallas_call(
        remix_kernel,
        grid=(rows // QB,),
        in_specs=[
            pl.BlockSpec((depth, rows), lambda i: (0, 0)),
            pl.BlockSpec((depth, BR), lambda i: (0, 0)),
            pl.BlockSpec((depth, BR), lambda i: (0, 0)),
            pl.BlockSpec((keys, QB), lambda i: (0, i)),
        ],
        out_specs=pl.BlockSpec((depth, QB), lambda i: (0, i)),
        out_shape=jax.ShapeDtypeStruct((depth, rows), F32),
        compiler_params=params(),
        cost_estimate=cost(2 * keys * rows * depth, 8 * depth * rows),
        name="remix",
    )(labels_t, below, above, powers)


def last_kernel(got_ref, p_ref, mix_ref, scale_ref, prior_ref, out_ref):
    relays, sub, near_keys = got_ref.shape
    near = nn(got_ref[...].reshape(relays * sub, near_keys), p_ref[...])
    mixed = mix_ref[...] * scale_ref[0:1] + near * scale_ref[1:2]
    sharp = sharpened(mixed, prior_ref)
    out_ref[...] = sharp * float(out_ref.shape[0])


def last_part(got, powers, mix, scales, prior_t):
    relays, sub, near_keys = got.shape
    classes, rows = prior_t.shape
    depth = relays * sub
    return pl.pallas_call(
        last_kernel,
        grid=(rows // QB,),
        in_specs=[
            pl.BlockSpec((relays, sub, near_keys), lambda i: (0, 0, 0)),
            pl.BlockSpec((near_keys, QB), lambda i: (0, i)),
            pl.BlockSpec((depth, QB), lambda i: (0, i)),
            pl.BlockSpec((8, QB), lambda i: (0, i)),
            pl.BlockSpec((classes, QB), lambda i: (0, i)),
        ],
        out_specs=pl.BlockSpec((classes, QB), lambda i: (0, i)),
        out_shape=jax.ShapeDtypeStruct((classes, rows), F32),
        compiler_params=params(),
        cost_estimate=cost(2 * near_keys * rows * depth, 12 * depth * rows),
        name="last_part",
    )(got, powers, mix, scales, prior_t)


def exchanged(x):
    return lax.all_to_all(x, "member", split_axis=0, concat_axis=0, tiled=True)


def body(embeddings, prior, source_member, source_block, cross_block, row_links):
    relays = lax.axis_size("member")
    groups = lax.axis_size("group")
    group = lax.axis_index("group")
    rows = embeddings.shape[0]
    owners, blocks = source_member[0], source_block[0]
    near_slots = owners.shape[1]
    prior_t, links_t = prior.T, row_links.T
    up = [(i, (i + 1) % groups) for i in range(groups)]
    down = [(j, i) for i, j in up]
    asked = cross_block[:, 0, :]
    to_above = lax.dynamic_slice(asked, ((group + 1) % groups, 0), (1, 1)).reshape(1)
    to_below = lax.dynamic_slice(asked, ((group + groups - 1) % groups, 1), (1, 1)).reshape(1)

    spread = prep(prior_t, embeddings, relays)
    relayed = exchanged(spread)
    below = lax.ppermute(pack(to_above, embeddings, spread), "group", up)
    above = lax.ppermute(pack(to_below, embeddings, spread), "group", down)
    far_powers, mix, stat = own_part(embeddings, spread, below, above, links_t, near_slots)
    near = exchanged(select(owners, blocks, relayed))
    labels_t, near_powers, scales = near_part(near, embeddings, links_t, mix, stat, prior_t)

    relayed = exchanged(labels_t.reshape(relays, SUB, rows))
    below = lax.ppermute(pack_labels(to_above, labels_t), "group", up)
    above = lax.ppermute(pack_labels(to_below, labels_t), "group", down)
    mix = remix(labels_t, below, above, far_powers)
    near = exchanged(select(owners, blocks, relayed))
    return last_part(near, near_powers, mix, scales, prior_t).T


def solution(mesh):
    placed = (
        P(("group", "member"), None),
        P(("group", "member"), None),
        P("group", None, None),
        P("group", None, None),
        P(None, "member", None),
        P(("group", "member"), None),
    )
    return jax.shard_map(
        body, mesh=mesh, in_specs=placed, out_specs=P(("group", "member"), None), check_vma=False
    )
```

profile of v0, /device:TPU:1, one launch (start us, length us, event | category | flops | bytes accessed | tf_op | source)
XLA Modules:
  0.0 171.5 jit_solution(5360364271779232527)
XLA Ops:
  0.0 0.0 copy-start
  0.0 1.9 %copy-done = f32[768,1000]{0,1:T(8,128)S(1)} copy-done((f32[768,1000]{0,1:T(8,128)S(1)}, f32[768,1000]{0,1:T(8,128)}, u32[]{:S(2)}) %copy-start) | copy-done | bytes 3072024
  1.9 0.0 copy-start.5
  1.9 1.4 copy-done.5
  3.3 3.4 %prep.1.lab_ref.refs_2_ = bf16[32,64,768]{2,1,0:T(8,128)(2,1)} custom-call(f32[1000,768]{1,0:T(8,128)S(1)} %bitcast.8, bf16[768,1024]{1,0:T(8,128)(2,1)S(1)} %copy-done.5), custom_call_target="tpu_custom_call" | custom-call | flops 3072000 | bytes 6217728 | tf_op jit(solution)/shard_map/prep/pallas_call | solution.py:57
  6.7 0.0 copy-start.20
  6.7 0.0 copy-start.21
  6.7 8.7 %all-to-all-start = ((bf16[32,64,768]{2,1,0:T(8,128)(2,1)}), bf16[32,64,768]{2,1,0:T(8,128)(2,1)S(1)}, u32[]{:S(2)}, u32[]{:S(2)}) async-start(bf16[32,64,768]{2,1,0:T(8,128)(2,1)} %prep.1.lab_ref.refs_2_), calls=%async_computation | async-start | bytes 6291456 | tf_op jit(solution)/shard_map/all_to_all | solution.py:355
  15.4 0.0 copy-done.20
  15.4 0.1 copy.10.block_ref
  15.5 0.0 copy-done.21
  15.5 0.1 copy.9.owner_ref
  15.6 39.0 %all-to-all-done.got_ref = bf16[32,64,768]{2,1,0:T(8,128)(2,1)S(1)} async-done(((bf16[32,64,768]{2,1,0:T(8,128)(2,1)}), bf16[32,64,768]{2,1,0:T(8,128)(2,1)S(1)}, u32[]{:S(2)}, u32[]{:S(2)}) %all-to-all-start) | async-done | bytes 3145760 | tf_op jit(solution)/shard_map/all_to_all | solution.py:355
  54.6 1.8 %select.6 = bf16[32,64,512]{2,1,0:T(8,128)(2,1)S(1)} custom-call(s32[32,4]{1,0:T(8,128)S(1)} %copy.9.owner_ref, s32[32,4]{1,0:T(8,128)S(1)} %copy.10.block_ref, bf16[32,64,768]{2,1,0:T(8,128)(2,1)S(1)} %all-to-all-done.got_ref), custom_call_target="tpu_custom_call" | custom-call | bytes 6291456 | tf_op jit(solution)/shard_map/select/pallas_call | solution.py:85
  56.4 0.0 copy-start.11
  56.4 1.3 copy-done.11
  57.7 7.3 %all-to-all-start.1 = ((bf16[32,64,512]{2,1,0:T(8,128)(2,1)}), bf16[32,64,512]{2,1,0:T(8,128)(2,1)}, u32[]{:S(2)}, u32[]{:S(2)}) async-start(bf16[32,64,512]{2,1,0:T(8,128)(2,1)} %copy-done.11), calls=%async_computation.1 | async-start | bytes 4194304 | tf_op jit(solution)/shard_map/all_to_all | solution.py:355
  65.1 0.0 copy-done.22
  65.1 0.6 constant_dynamic-slice_fusion
  65.7 0.0 copy-done.6
  65.7 1.6 pack_cross.2
  67.3 0.0 copy-start.7
  67.3 0.0 copy-start.19
  67.3 1.7 collective-permute-start
  69.0 1.7 pack_cross.3
  70.7 4.1 %collective-permute-start.1 = (bf16[256,1024]{1,0:T(8,128)(2,1)S(1)}, bf16[256,1024]{1,0:T(8,128)(2,1)S(1)}, u32[]{:S(2)}, u32[]{:S(2)}) collective-permute-start(bf16[256,1024]{1,0:T(8,128)(2,1)S(1)} %pack_cross.3), channel_id=1, source_target_pairs={{32,0},{64,32},{96,64},{128,96},{160,128},{192,160},{224,192},{0,2... | collective-permute-start | bytes 1572872 | tf_op jit(solution)/shard_map/ppermute | solution.py:375
  74.8 10.2 %collective-permute-done.refs_3_ = bf16[256,1024]{1,0:T(8,128)(2,1)S(1)} collective-permute-done((bf16[256,1024]{1,0:T(8,128)(2,1)S(1)}, bf16[256,1024]{1,0:T(8,128)(2,1)S(1)}, u32[]{:S(2)}, u32[]{:S(2)}) %collective-permute-start) | collective-permute-done | bytes 524320 | tf_op jit(solution)/shard_map/ppermute | solution.py:374
  85.0 0.7 collective-permute-done.1.refs_4_
  85.7 0.0 copy-done.7
  85.7 0.0 copy-done.19
  85.7 8.1 %own_part.1 = (bf16[1024,768]{1,0:T(8,128)(2,1)S(1)}, f32[1024,768]{1,0:T(8,128)S(1)}, f32[8,768]{1,0:T(8,128)S(1)}) custom-call(bf16[768,1024]{1,0:T(8,128)(2,1)S(1)} %copy-done.7, bf16[768,1024]{1,0:T(8,128)(2,1)S(1)} %copy-done.7, bf16[32,64,768]{2,1,0:T(8,128)(2,1)} %prep.1.lab_ref.refs_2_, bf16[256,1024]{1,0:T(8,128)(2,1)S(1)} %collective-permute-done.refs_3_, ...), custom_call_target="tpu_custom_call" | custom-call | flops 3221225472 | bytes 9437184 | tf_op jit(solution)/shard_map/own_part/pallas_call | solution.py:190
  93.8 0.0 copy-start.13
  93.9 1.6 copy-done.13
  95.5 1.2 copy-done.15
  96.7 0.0 all-to-all-done.1.got_ref
  96.7 0.0 copy-done.1
  96.7 1.4 copy-done.8
  98.1 1.9 %copy-done.14 = f32[1024,768]{1,0:T(8,128)S(1)} copy-done((f32[1024,768]{1,0:T(8,128)S(1)}, f32[1024,768]{1,0:T(8,128)}, u32[]{:S(2)}) %copy-start.14) | copy-done | bytes 3145752
  100.0 7.1 %near_part.1 = (bf16[1024,768]{1,0:T(8,128)(2,1)S(1)}, bf16[512,768]{1,0:T(8,128)(2,1)S(1)}, f32[8,768]{1,0:T(8,128)S(1)}) custom-call(bf16[32,64,512]{2,1,0:T(8,128)(2,1)} %all-to-all-done.1.got_ref, bf16[768,1024]{1,0:T(8,128)(2,1)S(1)} %copy-done.8, s32[4,768]{1,0:T(4,128)S(1)} %bitcast.13, f32[1024,768]{1,0:T(8,128)S(1)} %copy-done.14, ...), custom_call_target="tpu_custom_call" | custom-call | flops 1610612736 | bytes 9437184 | tf_op jit(solution)/shard_map/near_part/pallas_call | solution.py:270
  107.1 0.0 copy-start.17
  107.1 31.0 %all_to_all.20.got_ref = bf16[32,32,768]{2,1,0:T(8,128)(2,1)S(1)} all-to-all(bf16[32,32,768]{2,1,0:T(8,128)(2,1)S(1)} %bitcast.11), channel_id=1, replica_groups=mesh['group'=8,'member'=32] {'member'}, dimensions={0} | all-to-all | bytes 3145728 | tf_op jit(solution)/shard_map/all_to_all | solution.py:355
  138.1 0.0 copy-done.17
  138.1 1.1 copy-done.2
  139.2 1.6 select.7
  140.8 0.0 copy-start.12
  140.8 1.0 copy-done.12
  141.9 4.7 %all-to-all-start.3 = ((bf16[32,32,512]{2,1,0:T(8,128)(2,1)}), bf16[32,32,512]{2,1,0:T(8,128)(2,1)}, u32[]{:S(2)}, u32[]{:S(2)}) async-start(bf16[32,32,512]{2,1,0:T(8,128)(2,1)} %copy-done.12), calls=%async_computation.3 | async-start | bytes 2097152 | tf_op jit(solution)/shard_map/all_to_all | solution.py:355
  146.5 0.0 copy-start.3
  146.6 1.4 copy-done.3
  148.0 0.8 pack_labels.2
  148.7 0.9 pack_labels.3
  149.6 0.1 collective-permute-start.2
  149.7 3.5 %collective-permute-start.3 = (bf16[1024,128]{1,0:T(8,128)(2,1)S(1)}, bf16[1024,128]{1,0:T(8,128)(2,1)S(1)}, u32[]{:S(2)}, u32[]{:S(2)}) collective-permute-start(bf16[1024,128]{1,0:T(8,128)(2,1)S(1)} %pack_labels.3), channel_id=1, source_target_pairs={{32,0},{64,32},{96,64},{128,96},{160,128},{192,160},{224,192},{0,2... | collective-permute-start | bytes 786440 | tf_op jit(solution)/shard_map/ppermute | solution.py:382
  153.2 6.3 %collective-permute-done.2.below_ref = bf16[1024,128]{1,0:T(8,128)(2,1)S(1)} collective-permute-done((bf16[1024,128]{1,0:T(8,128)(2,1)S(1)}, bf16[1024,128]{1,0:T(8,128)(2,1)S(1)}, u32[]{:S(2)}, u32[]{:S(2)}) %collective-permute-start.2) | collective-permute-done | bytes 262176 | tf_op jit(solution)/shard_map/ppermute | solution.py:381
  159.6 0.0 collective-permute-done.3.above_ref
  159.6 0.0 copy-done.4
  159.6 0.0 copy-done.16
  159.6 2.5 %remix.1.mix_ref = f32[1024,768]{1,0:T(8,128)S(1)} custom-call(bf16[1024,768]{1,0:T(8,128)(2,1)S(1)} %copy-done.4, bf16[1024,128]{1,0:T(8,128)(2,1)S(1)} %collective-permute-done.2.below_ref, bf16[1024,128]{1,0:T(8,128)(2,1)S(1)} %collective-permute-done.3.above_ref, bf16[1024,768]{1,0:T(8,128)(2,1)S(1)} %copy-done.16), custom_call_target="tpu_custom_call" | custom-call | flops 1610612736 | bytes 6291456 | tf_op jit(solution)/shard_map/remix/pallas_call | solution.py:307
  162.0 0.0 copy-start.9
  162.0 1.6 copy-done.9
  163.7 0.2 all-to-all-done.3.got_ref
  163.9 1.9 %copy-done.10 = f32[1024,768]{1,0:T(8,128)S(1)} copy-done((f32[1024,768]{1,0:T(8,128)S(1)}, f32[1024,768]{1,0:T(8,128)}, u32[]{:S(2)}) %copy-start.10) | copy-done | bytes 3145752
  165.8 1.1 copy-done.18
  166.9 4.6 %last_part.1 = f32[1000,768]{1,0:T(8,128)} custom-call(bf16[32,32,512]{2,1,0:T(8,128)(2,1)} %all-to-all-done.3.got_ref, bf16[512,768]{1,0:T(8,128)(2,1)S(1)} %copy-done.18, f32[1024,768]{1,0:T(8,128)S(1)} %copy-done.10, f32[8,768]{1,0:T(8,128)S(1)} %get-tuple-element.16.scale_ref, f32[1000,768]{1,0:T(8,128)S(1)} %bitcast.10), custom_call_target="tpu_custom_call" | custom-call | flops 805306368 | bytes 9437184 | tf_op jit(solution)/shard_map/last_part/pallas_call | solution.py:336
  (11 shorter events, 0.0 us)
Async XLA Ops:
  0.0 1.9 %copy-start = (f32[768,1000]{0,1:T(8,128)S(1)}, f32[768,1000]{0,1:T(8,128)}, u32[]{:S(2)}) copy-start(f32[768,1000]{0,1:T(8,128)} %param.7) | copy-start | bytes 9216004
  1.9 1.4 copy-start.5
  6.7 8.7 %copy-start.20 = (s32[1,32,4]{1,2,0:T(4,128)S(1)}, s32[1,32,4]{1,2,0:T(4,128)}, u32[]{:S(2)}) copy-start(s32[1,32,4]{1,2,0:T(4,128)} %param.9) | copy-start | bytes 1540
  6.7 8.8 %copy-start.21 = (s32[1,32,4]{1,2,0:T(4,128)S(1)}, s32[1,32,4]{1,2,0:T(4,128)}, u32[]{:S(2)}) copy-start(s32[1,32,4]{1,2,0:T(4,128)} %param.8) | copy-start | bytes 1540
  6.7 47.9 %all-to-all-start = ((bf16[32,64,768]{2,1,0:T(8,128)(2,1)}), bf16[32,64,768]{2,1,0:T(8,128)(2,1)S(1)}, u32[]{:S(2)}, u32[]{:S(2)}) async-start(bf16[32,64,768]{2,1,0:T(8,128)(2,1)} %prep.1.lab_ref.refs_2_), calls=%async_computation | async-start | bytes 6291456 | tf_op jit(solution)/shard_map/all_to_all | solution.py:355
  56.4 1.3 copy-start.11
  57.7 7.3 %copy-start.22 = (s32[8,1,2]{0,2,1:T(2,128)S(1)}, s32[8,1,2]{0,2,1:T(2,128)}, u32[]{:S(2)}) copy-start(s32[8,1,2]{0,2,1:T(2,128)} %param.10) | copy-start | bytes 196
  57.7 8.0 %copy-start.6 = (bf16[768,1024]{1,0:T(8,128)(2,1)S(1)}, bf16[768,1024]{1,0:T(8,128)(2,1)}, u32[]{:S(2)}) copy-start(bf16[768,1024]{1,0:T(8,128)(2,1)} %q_ref.1) | copy-start | bytes 4718596
  57.7 38.9 %all-to-all-start.1 = ((bf16[32,64,512]{2,1,0:T(8,128)(2,1)}), bf16[32,64,512]{2,1,0:T(8,128)(2,1)}, u32[]{:S(2)}, u32[]{:S(2)}) async-start(bf16[32,64,512]{2,1,0:T(8,128)(2,1)} %copy-done.11), calls=%async_computation.1 | async-start | bytes 4194304 | tf_op jit(solution)/shard_map/all_to_all | solution.py:355
  67.3 18.4 %copy-start.7 = (bf16[768,1024]{1,0:T(8,128)(2,1)S(1)}, bf16[768,1024]{1,0:T(8,128)(2,1)}, u32[]{:S(2)}) copy-start(bf16[768,1024]{1,0:T(8,128)(2,1)} %q_ref.1) | copy-start | bytes 4718596
  67.3 18.4 %copy-start.19 = (s32[768,4]{0,1:T(4,128)S(1)}, s32[768,4]{0,1:T(4,128)}, u32[]{:S(2)}) copy-start(s32[768,4]{0,1:T(4,128)} %param.11) | copy-start | bytes 36868
  67.3 17.7 %collective-permute-start = (bf16[256,1024]{1,0:T(8,128)(2,1)S(1)}, bf16[256,1024]{1,0:T(8,128)(2,1)S(1)}, u32[]{:S(2)}, u32[]{:S(2)}) collective-permute-start(bf16[256,1024]{1,0:T(8,128)(2,1)S(1)} %pack_cross.2), channel_id=1, source_target_pairs={{0,32},{32,64},{64,96},{96,128},{128,160},{160,192},{192,224},{224... | collective-permute-start | bytes 1572872 | tf_op jit(solution)/shard_map/ppermute | solution.py:374
  70.7 15.0 %collective-permute-start.1 = (bf16[256,1024]{1,0:T(8,128)(2,1)S(1)}, bf16[256,1024]{1,0:T(8,128)(2,1)S(1)}, u32[]{:S(2)}, u32[]{:S(2)}) collective-permute-start(bf16[256,1024]{1,0:T(8,128)(2,1)S(1)} %pack_cross.3), channel_id=1, source_target_pairs={{32,0},{64,32},{96,64},{128,96},{160,128},{192,160},{224,192},{0,2... | collective-permute-start | bytes 1572872 | tf_op jit(solution)/shard_map/ppermute | solution.py:375
  85.7 11.0 %copy-start.1 = (f32[768,1000]{0,1:T(8,128)S(1)}, f32[768,1000]{0,1:T(8,128)}, u32[]{:S(2)}) copy-start(f32[768,1000]{0,1:T(8,128)} %param.7) | copy-start | bytes 9216004
  93.8 1.6 copy-start.13
  95.5 1.2 copy-start.15
  96.7 1.4 copy-start.8
  98.1 1.9 %copy-start.14 = (f32[1024,768]{1,0:T(8,128)S(1)}, f32[1024,768]{1,0:T(8,128)}, u32[]{:S(2)}) copy-start(f32[1024,768]{1,0:T(8,128)} %copy-done.13) | copy-start | bytes 9437188
  107.1 31.0 %copy-start.17 = (bf16[512,768]{1,0:T(8,128)(2,1)}, bf16[512,768]{1,0:T(8,128)(2,1)S(1)}, u32[]{:S(2)}) copy-start(bf16[512,768]{1,0:T(8,128)(2,1)S(1)} %get-tuple-element.14.p_ref) | copy-start | bytes 2359300
  138.1 1.1 copy-start.2
  140.8 1.0 copy-start.12
  141.9 22.0 %all-to-all-start.3 = ((bf16[32,32,512]{2,1,0:T(8,128)(2,1)}), bf16[32,32,512]{2,1,0:T(8,128)(2,1)}, u32[]{:S(2)}, u32[]{:S(2)}) async-start(bf16[32,32,512]{2,1,0:T(8,128)(2,1)} %copy-done.12), calls=%async_computation.3 | async-start | bytes 2097152 | tf_op jit(solution)/shard_map/all_to_all | solution.py:355
  146.5 1.4 copy-start.3
  148.0 11.6 %copy-start.4 = (bf16[1024,768]{1,0:T(8,128)(2,1)S(1)}, bf16[1024,768]{1,0:T(8,128)(2,1)}, u32[]{:S(2)}) copy-start(bf16[1024,768]{1,0:T(8,128)(2,1)} %copy-done.2) | copy-start | bytes 4718596
  148.0 11.6 %copy-start.16 = (bf16[1024,768]{1,0:T(8,128)(2,1)S(1)}, bf16[1024,768]{1,0:T(8,128)(2,1)}, u32[]{:S(2)}) copy-start(bf16[1024,768]{1,0:T(8,128)(2,1)} %copy-done.15) | copy-start | bytes 4718596
  149.6 9.9 %collective-permute-start.2 = (bf16[1024,128]{1,0:T(8,128)(2,1)S(1)}, bf16[1024,128]{1,0:T(8,128)(2,1)S(1)}, u32[]{:S(2)}, u32[]{:S(2)}) collective-permute-start(bf16[1024,128]{1,0:T(8,128)(2,1)S(1)} %pack_labels.2), channel_id=1, source_target_pairs={{0,32},{32,64},{64,96},{96,128},{128,160},{160,192},{192,224},{224... | collective-permute-start | bytes 786440 | tf_op jit(solution)/shard_map/ppermute | solution.py:381
  149.7 9.9 %collective-permute-start.3 = (bf16[1024,128]{1,0:T(8,128)(2,1)S(1)}, bf16[1024,128]{1,0:T(8,128)(2,1)S(1)}, u32[]{:S(2)}, u32[]{:S(2)}) collective-permute-start(bf16[1024,128]{1,0:T(8,128)(2,1)S(1)} %pack_labels.3), channel_id=1, source_target_pairs={{32,0},{64,32},{96,64},{128,96},{160,128},{192,160},{224,192},{0,2... | collective-permute-start | bytes 786440 | tf_op jit(solution)/shard_map/ppermute | solution.py:382
  162.0 1.6 copy-start.9
  163.9 1.9 %copy-start.10 = (f32[1024,768]{1,0:T(8,128)S(1)}, f32[1024,768]{1,0:T(8,128)}, u32[]{:S(2)}) copy-start(f32[1024,768]{1,0:T(8,128)} %copy-done.9) | copy-start | bytes 9437188
  165.8 1.1 copy-start.18
where the time goes:
time: 172 us
  waiting for transfers between devices  56.4 us (33%)
  Pallas kernels  34 us (20%)
  blocking collectives  31 us (18%)
  starting transfers between devices  30.1 us (18%)
  local copies, waits for them, and re-layouts  19.7 us (11%)
    all_to_all x3, waiting for transfers between devices, exchanged(): return lax.all_to_all(x, 'member', split_axis=0, concat_axis=0, tiled=True)  39.2 us
    all_to_all x1, blocking collectives, exchanged(): return lax.all_to_all(x, 'member', split_axis=0, concat_axis=0, tiled=True)  31 us
    all_to_all x3, starting transfers between devices, exchanged(): return lax.all_to_all(x, 'member', split_axis=0, concat_axis=0, tiled=True)  20.7 us
    unnamed x46, local copies, waits for them, and re-layouts  19 us
    ppermute x1, waiting for transfers between devices, body(): below = lax.ppermute(pack(to_above, embeddings, spread), 'group', up)  10.2 us
    pallas_call x1, Pallas kernels, own_part(): pl.pallas_call(lambda *refs: own_kernel(near_slots, *refs), grid=(rows //...  8.13 us
    pallas_call x1, Pallas kernels, near_part(): pl.pallas_call(near_kernel, grid=(rows // QB,), in_specs=[pl.BlockSpec((r...  7.14 us
    ppermute x1, waiting for transfers between devices, body(): below = lax.ppermute(pack_labels(to_above, labels_t), 'group', up)  6.34 us
  transfers between devices with their start and end apart: 7, of which 5 were waited for; matrix products, arithmetic and copies ran while one was open for 0% of the time, Pallas kernels for 9%

commit v1 on v0

--- a/solution.py
+++ b/solution.py
@@ -18,6 +18,10 @@
     return pltpu.CompilerParams(
         dimension_semantics=("arbitrary",), vmem_limit_bytes=VMEM_BYTES
     )
+
+
+def in_hbm(x):
+    return pltpu.with_memory_space_constraint(x, pltpu.HBM)
 
 
 def cost(flops, size, exps=0):
@@ -66,10 +70,10 @@
         compiler_params=params(),
         cost_estimate=cost(4 * classes * rows, 4 * classes * rows + 4 * features * rows),
         name="prep",
-    )(prior_t, emb)
-
-
-def select_kernel(owner_ref, block_ref, got_ref, out_ref):
+    )(in_hbm(prior_t), in_hbm(emb))
+
+
+def select_kernel(owner_ref, block_ref, got_ref, after_ref, out_ref):
     members, slots = owner_ref.shape
 
     @pl.loop(0, members)
@@ -79,7 +83,7 @@
             out_ref[d, :, k * BR : (k + 1) * BR] = got_ref[owner_ref[d, k], :, pl.ds(lane, BR)]
 
 
-def select(owners, blocks, got):
+def select(owners, blocks, got, after):
     members, slots = owners.shape
     depth = got.shape[1]
     return pl.pallas_call(
@@ -88,13 +92,14 @@
             pl.BlockSpec(memory_space=pltpu.SMEM),
             pl.BlockSpec(memory_space=pltpu.SMEM),
             pl.BlockSpec(memory_space=pltpu.VMEM),
+            pl.BlockSpec(memory_space=pl.ANY),
         ],
         out_specs=pl.BlockSpec(memory_space=pltpu.VMEM),
         out_shape=jax.ShapeDtypeStruct((members, depth, slots * BR), BF),
         compiler_params=pltpu.CompilerParams(vmem_limit_bytes=VMEM_BYTES),
         cost_estimate=cost(0, 4 * got.size),
         name="select",
-    )(owners, blocks, got)
+    )(owners, blocks, got, after)
 
 
 def pack_kernel(pick_ref, emb_ref, lab_ref, out_ref):
@@ -374,14 +379,14 @@
     below = lax.ppermute(pack(to_above, embeddings, spread), "group", up)
     above = lax.ppermute(pack(to_below, embeddings, spread), "group", down)
     far_powers, mix, stat = own_part(embeddings, spread, below, above, links_t, near_slots)
-    near = exchanged(select(owners, blocks, relayed))
+    near = exchanged(select(owners, blocks, relayed, stat))
     labels_t, near_powers, scales = near_part(near, embeddings, links_t, mix, stat, prior_t)
 
     relayed = exchanged(labels_t.reshape(relays, SUB, rows))
     below = lax.ppermute(pack_labels(to_above, labels_t), "group", up)
     above = lax.ppermute(pack_labels(to_below, labels_t), "group", down)
     mix = remix(labels_t, below, above, far_powers)
-    near = exchanged(select(owners, blocks, relayed))
+    near = exchanged(select(owners, blocks, relayed, mix))
     return last_part(near, near_powers, mix, scales, prior_t).T
 
 

time: 172 us -> 156 us (0.907)
  waiting for transfers between devices: 56.4 us -> 27.5 us
  blocking collectives: 31 us -> 58.9 us
  local copies, waits for them, and re-layouts: 19.7 us -> 4.6 us
  Pallas kernels: 34 us -> 39.6 us
  starting transfers between devices: 30.1 us -> 24.8 us
    all_to_all x3 -> x2, waiting for transfers between devices: 39.2 us -> 4.99 us  [exchanged(): return lax.all_to_all(x, 'member', split_axis=0, concat_axis=0, tiled=True)]
    all_to_all x1 -> x2, blocking collectives: 31 us -> 58.9 us  [exchanged(): return lax.all_to_all(x, 'member', split_axis=0, concat_axis=0, tiled=True)]
    unnamed x46 -> x26, local copies, waits for them, and re-layouts: 19 us -> 3.76 us
    ppermute x1, waiting for transfers between devices: 0.7 us -> 9.08 us  [body(): above = lax.ppermute(pack(to_below, embeddings, spread), 'group', down)]
    all_to_all x3 -> x2, starting transfers between devices: 20.7 us -> 13.5 us  [exchanged(): return lax.all_to_all(x, 'member', split_axis=0, concat_axis=0, tiled=True)]
    ppermute x1, waiting for transfers between devices: 0.01 us -> 5.27 us  [body(): above = lax.ppermute(pack_labels(to_below, labels_t), 'group', down)]
    ppermute x1, waiting for transfers between devices: 10.2 us -> 4.93 us  [body(): below = lax.ppermute(pack(to_above, embeddings, spread), 'group', up)]
    ppermute x1, waiting for transfers between devices: 6.34 us -> 3.19 us  [body(): below = lax.ppermute(pack_labels(to_above, labels_t), 'group', up)]
  transfers between devices with their start and end apart: 7 -> 6, of which waited for: 5 -> 6; matrix products, arithmetic and copies ran while one was open for 0% -> 1% of each run, Pallas kernels for 9% -> 12%
where the time goes in v1:
time: 156 us
  blocking collectives  58.9 us (38%)
  Pallas kernels  39.6 us (25%)
  waiting for transfers between devices  27.5 us (18%)
  starting transfers between devices  24.8 us (16%)
  local copies, waits for them, and re-layouts  4.6 us (3%)
    all_to_all x2, blocking collectives, exchanged(): return lax.all_to_all(x, 'member', split_axis=0, concat_axis=0, tiled=True)  58.9 us
    all_to_all x2, starting transfers between devices, exchanged(): return lax.all_to_all(x, 'member', split_axis=0, concat_axis=0, tiled=True)  13.5 us
    ppermute x1, waiting for transfers between devices, body(): above = lax.ppermute(pack(to_below, embeddings, spread), 'group', down)  9.08 us
    pallas_call x1, Pallas kernels, own_part(): pl.pallas_call(lambda *refs: own_kernel(near_slots, *refs), grid=(rows //...  8.25 us
    pallas_call x1, Pallas kernels, near_part(): pl.pallas_call(near_kernel, grid=(rows // QB,), in_specs=[pl.BlockSpec((r...  6.48 us
    pallas_call x1, Pallas kernels, prep(): pl.pallas_call(prep_kernel, grid=(rows // BR,), in_specs=[pl.BlockSpec((c...  6.02 us
    ppermute x1, starting transfers between devices, body(): above = lax.ppermute(pack(to_below, embeddings, spread), 'group', down)  5.65 us
    ppermute x1, starting transfers between devices, body(): above = lax.ppermute(pack_labels(to_below, labels_t), 'group', down)  5.65 us
  transfers between devices with their start and end apart: 6, of which 6 were waited for; matrix products, arithmetic and copies ran while one was open for 1% of the time, Pallas kernels for 12%

profile of v1, /device:TPU:1, one launch (start us, length us, event | category | flops | bytes accessed | tf_op | source)
XLA Modules:
  0.0 155.7 jit_solution(15220260466120050882)
XLA Ops:
  0.0 6.0 %prep.1.lab_ref.refs_2_ = bf16[32,64,768]{2,1,0:T(8,128)(2,1)} custom-call(f32[1000,768]{1,0:T(8,128)} %bitcast.8, bf16[768,1024]{1,0:T(8,128)(2,1)} %q_ref.1), custom_call_target="tpu_custom_call" | custom-call | flops 3072000 | bytes 6217728 | tf_op jit(solution)/shard_map/prep/pallas_call | solution.py:61
  6.0 0.0 copy-start.12
  6.0 0.0 copy-start.2
  6.0 8.8 %all-to-all-start = ((bf16[32,64,768]{2,1,0:T(8,128)(2,1)}), bf16[32,64,768]{2,1,0:T(8,128)(2,1)}, u32[]{:S(2)}, u32[]{:S(2)}) async-start(bf16[32,64,768]{2,1,0:T(8,128)(2,1)} %prep.1.lab_ref.refs_2_), calls=%async_computation | async-start | bytes 6291456 | tf_op jit(solution)/shard_map/all_to_all | solution.py:360
  14.8 0.0 copy-done.12
  14.8 0.7 constant_dynamic-slice_fusion
  15.5 0.0 copy-done.2
  15.5 1.7 %pack_cross.3 = bf16[256,1024]{1,0:T(8,128)(2,1)S(1)} custom-call(s32[1]{0:T(128)} %bitcast.4.pick_ref, bf16[768,1024]{1,0:T(8,128)(2,1)S(1)} %copy-done.2, bf16[32,64,768]{2,1,0:T(8,128)(2,1)} %prep.1.lab_ref.refs_2_), custom_call_target="tpu_custom_call" | custom-call | bytes 1048576 | tf_op jit(solution)/shard_map/pack_cross/pallas_call | solution.py:115
  17.3 0.0 copy-start.10
  17.3 0.0 copy-start.11
  17.3 0.0 copy-start.9
  17.3 5.7 %collective-permute-start.1 = (bf16[256,1024]{1,0:T(8,128)(2,1)S(1)}, bf16[256,1024]{1,0:T(8,128)(2,1)}, u32[]{:S(2)}, u32[]{:S(2)}) collective-permute-start(bf16[256,1024]{1,0:T(8,128)(2,1)S(1)} %pack_cross.3), channel_id=1, source_target_pairs={{32,0},{64,32},{96,64},{128,96},{160,128},{192,160},{224,192},{0,2... | collective-permute-start | bytes 1572872 | tf_op jit(solution)/shard_map/ppermute | solution.py:380
  22.9 1.7 %pack_cross.2 = bf16[256,1024]{1,0:T(8,128)(2,1)S(1)} custom-call(s32[1]{0:T(128)} %bitcast.3.pick_ref, bf16[768,1024]{1,0:T(8,128)(2,1)S(1)} %copy-done.2, bf16[32,64,768]{2,1,0:T(8,128)(2,1)} %prep.1.lab_ref.refs_2_), custom_call_target="tpu_custom_call" | custom-call | bytes 1048576 | tf_op jit(solution)/shard_map/pack_cross/pallas_call | solution.py:115
  24.6 0.1 collective-permute-start
  24.7 0.0 copy-done.10
  24.7 0.1 copy.10.block_ref
  24.8 0.0 copy-done.11
  24.8 0.1 copy.9.owner_ref
  24.9 9.1 %collective-permute-done.1.refs_4_ = bf16[256,1024]{1,0:T(8,128)(2,1)} collective-permute-done((bf16[256,1024]{1,0:T(8,128)(2,1)S(1)}, bf16[256,1024]{1,0:T(8,128)(2,1)}, u32[]{:S(2)}, u32[]{:S(2)}) %collective-permute-start.1) | collective-permute-done | bytes 524320 | tf_op jit(solution)/shard_map/ppermute | solution.py:380
  34.0 4.9 %collective-permute-done.refs_3_ = bf16[256,1024]{1,0:T(8,128)(2,1)} collective-permute-done((bf16[256,1024]{1,0:T(8,128)(2,1)S(1)}, bf16[256,1024]{1,0:T(8,128)(2,1)}, u32[]{:S(2)}, u32[]{:S(2)}) %collective-permute-start) | collective-permute-done | bytes 524320 | tf_op jit(solution)/shard_map/ppermute | solution.py:379
  38.9 0.0 copy-done.9
  38.9 8.3 %own_part.1 = (bf16[1024,768]{1,0:T(8,128)(2,1)S(1)}, f32[1024,768]{1,0:T(8,128)S(1)}, f32[8,768]{1,0:T(8,128)S(1)}) custom-call(bf16[768,1024]{1,0:T(8,128)(2,1)S(1)} %copy-done.2, bf16[768,1024]{1,0:T(8,128)(2,1)S(1)} %copy-done.2, bf16[32,64,768]{2,1,0:T(8,128)(2,1)} %prep.1.lab_ref.refs_2_, bf16[256,1024]{1,0:T(8,128)(2,1)} %collective-permute-done.refs_3_, ...), custom_call_target="tpu_custom_call" | custom-call | flops 3221225472 | bytes 9437184 | tf_op jit(solution)/shard_map/own_part/pallas_call | solution.py:195
  47.2 0.0 copy-start.3
  47.2 1.7 %copy-done.3 = f32[1024,768]{1,0:T(8,128)} copy-done((f32[1024,768]{1,0:T(8,128)}, f32[1024,768]{1,0:T(8,128)S(1)}, u32[]{:S(2)}) %copy-start.3) | copy-done | bytes 3145752
  48.9 0.0 copy-start.5
  48.9 1.1 copy-done.5
  50.0 4.0 %all-to-all-done.got_ref = bf16[32,64,768]{2,1,0:T(8,128)(2,1)} async-done(((bf16[32,64,768]{2,1,0:T(8,128)(2,1)}), bf16[32,64,768]{2,1,0:T(8,128)(2,1)}, u32[]{:S(2)}, u32[]{:S(2)}) %all-to-all-start) | async-done | bytes 3145760 | tf_op jit(solution)/shard_map/all_to_all | solution.py:360
  54.0 0.0 copy-start.4
  54.0 2.7 %select.6 = bf16[32,64,512]{2,1,0:T(8,128)(2,1)S(1)} custom-call(s32[32,4]{1,0:T(8,128)S(1)} %copy.9.owner_ref, s32[32,4]{1,0:T(8,128)S(1)} %copy.10.block_ref, bf16[32,64,768]{2,1,0:T(8,128)(2,1)} %all-to-all-done.got_ref, f32[8,768]{1,0:T(8,128)S(1)} %get-tuple-element.11.after_ref.stat_ref), custom_call_target="tpu_custom_call" | custom-call | bytes 6291456 | tf_op jit(solution)/shard_map/select/pallas_call | solution.py:89
  56.8 0.0 copy-start
  56.8 34.3 %all_to_all.20.got_ref = bf16[32,64,512]{2,1,0:T(8,128)(2,1)S(1)} all-to-all(bf16[32,64,512]{2,1,0:T(8,128)(2,1)S(1)} %select.6), channel_id=1, replica_groups=mesh['group'=8,'member'=32] {'member'}, dimensions={0} | all-to-all | bytes 4194304 | tf_op jit(solution)/shard_map/all_to_all | solution.py:360
  91.1 0.0 copy-done.4
  91.1 0.0 copy-done
  91.1 6.5 %near_part.1 = (bf16[1024,768]{1,0:T(8,128)(2,1)}, bf16[512,768]{1,0:T(8,128)(2,1)S(1)}, f32[8,768]{1,0:T(8,128)S(1)}) custom-call(bf16[32,64,512]{2,1,0:T(8,128)(2,1)S(1)} %all_to_all.20.got_ref, bf16[768,1024]{1,0:T(8,128)(2,1)S(1)} %copy-done.2, s32[4,768]{1,0:T(4,128)S(1)} %bitcast.12, f32[1024,768]{1,0:T(8,128)S(1)} %copy-done.4, ...), custom_call_target="tpu_custom_call" | custom-call | flops 1610612736 | bytes 9437184 | tf_op jit(solution)/shard_map/near_part/pallas_call | solution.py:275
  97.6 0.0 copy-start.7
  97.6 0.9 copy-done.7
  98.4 4.7 %all-to-all-start.2 = ((bf16[32,32,768]{2,1,0:T(8,128)(2,1)}), bf16[32,32,768]{2,1,0:T(8,128)(2,1)}, u32[]{:S(2)}, u32[]{:S(2)}) async-start(bf16[32,32,768]{2,1,0:T(8,128)(2,1)} %bitcast.6), calls=%async_computation.2 | async-start | bytes 3145728 | tf_op jit(solution)/shard_map/all_to_all | solution.py:360
  103.1 0.0 copy-start.6
  103.1 1.8 %pack_labels.3 = bf16[1024,128]{1,0:T(8,128)(2,1)S(1)} custom-call(s32[1]{0:T(128)} %bitcast.4.pick_ref, bf16[1024,768]{1,0:T(8,128)(2,1)} %get-tuple-element.13.lab_ref), custom_call_target="tpu_custom_call" | custom-call | bytes 524288 | tf_op jit(solution)/shard_map/pack_labels/pallas_call | solution.py:139
  104.9 1.6 %pack_labels.2 = bf16[1024,128]{1,0:T(8,128)(2,1)S(1)} custom-call(s32[1]{0:T(128)} %bitcast.3.pick_ref, bf16[1024,768]{1,0:T(8,128)(2,1)} %get-tuple-element.13.lab_ref), custom_call_target="tpu_custom_call" | custom-call | bytes 524288 | tf_op jit(solution)/shard_map/pack_labels/pallas_call | solution.py:139
  106.5 5.7 %collective-permute-start.3 = (bf16[1024,128]{1,0:T(8,128)(2,1)S(1)}, bf16[1024,128]{1,0:T(8,128)(2,1)S(1)}, u32[]{:S(2)}, u32[]{:S(2)}) collective-permute-start(bf16[1024,128]{1,0:T(8,128)(2,1)S(1)} %pack_labels.3), channel_id=1, source_target_pairs={{32,0},{64,32},{96,64},{128,96},{160,128},{192,160},{224,192},{0,2... | collective-permute-start | bytes 786440 | tf_op jit(solution)/shard_map/ppermute | solution.py:387
  112.1 0.0 collective-permute-start.2
  112.2 5.3 %collective-permute-done.3.above_ref = bf16[1024,128]{1,0:T(8,128)(2,1)S(1)} collective-permute-done((bf16[1024,128]{1,0:T(8,128)(2,1)S(1)}, bf16[1024,128]{1,0:T(8,128)(2,1)S(1)}, u32[]{:S(2)}, u32[]{:S(2)}) %collective-permute-start.3) | collective-permute-done | bytes 262176 | tf_op jit(solution)/shard_map/ppermute | solution.py:387
  117.4 3.2 %collective-permute-done.2.below_ref = bf16[1024,128]{1,0:T(8,128)(2,1)S(1)} collective-permute-done((bf16[1024,128]{1,0:T(8,128)(2,1)S(1)}, bf16[1024,128]{1,0:T(8,128)(2,1)S(1)}, u32[]{:S(2)}, u32[]{:S(2)}) %collective-permute-start.2) | collective-permute-done | bytes 262176 | tf_op jit(solution)/shard_map/ppermute | solution.py:386
  120.6 0.0 copy-done.6
  120.6 3.8 %remix.1.after_ref.mix_ref = f32[1024,768]{1,0:T(8,128)S(1)} custom-call(bf16[1024,768]{1,0:T(8,128)(2,1)} %get-tuple-element.13.lab_ref, bf16[1024,128]{1,0:T(8,128)(2,1)S(1)} %collective-permute-done.2.below_ref, bf16[1024,128]{1,0:T(8,128)(2,1)S(1)} %collective-permute-done.3.above_ref, bf16[1024,768]{1,0:T(8,128)(2,1)S(1)} %copy-done.6), custom_call_target="tpu_custom_call" | custom-call | flops 1610612736 | bytes 6291456 | tf_op jit(solution)/shard_map/remix/pallas_call | solution.py:312
  124.4 1.0 all-to-all-done.2.got_ref
  125.4 0.0 copy-start.1
  125.4 0.0 copy-start.8
  125.4 2.1 %select.7 = bf16[32,32,512]{2,1,0:T(8,128)(2,1)S(1)} custom-call(s32[32,4]{1,0:T(8,128)S(1)} %copy.9.owner_ref, s32[32,4]{1,0:T(8,128)S(1)} %copy.10.block_ref, bf16[32,32,768]{2,1,0:T(8,128)(2,1)} %all-to-all-done.2.got_ref, f32[1024,768]{1,0:T(8,128)S(1)} %remix.1.after_ref.mix_ref), custom_call_target="tpu_custom_call" | custom-call | bytes 3145728 | tf_op jit(solution)/shard_map/select/pallas_call | solution.py:89
  127.5 24.6 %all_to_all.21.got_ref = bf16[32,32,512]{2,1,0:T(8,128)(2,1)S(1)} all-to-all(bf16[32,32,512]{2,1,0:T(8,128)(2,1)S(1)} %select.7), channel_id=1, replica_groups=mesh['group'=8,'member'=32] {'member'}, dimensions={0} | all-to-all | bytes 2097152 | tf_op jit(solution)/shard_map/all_to_all | solution.py:360
  152.1 0.0 copy-done.1
  152.1 0.0 copy-done.8
  152.1 3.5 %last_part.1 = f32[1000,768]{1,0:T(8,128)} custom-call(bf16[32,32,512]{2,1,0:T(8,128)(2,1)S(1)} %all_to_all.21.got_ref, bf16[512,768]{1,0:T(8,128)(2,1)S(1)} %copy-done.8, f32[1024,768]{1,0:T(8,128)S(1)} %remix.1.after_ref.mix_ref, f32[8,768]{1,0:T(8,128)S(1)} %get-tuple-element.16.scale_ref, f32[1000,768]{1,0:T(8,128)S(1)} %bitcast.10), custom_call_target="tpu_custom_call" | custom-call | flops 805306368 | bytes 9437184 | tf_op jit(solution)/shard_map/last_part/pallas_call | solution.py:341
Async XLA Ops:
  6.0 8.8 %copy-start.12 = (s32[8,1,2]{0,2,1:T(2,128)S(1)}, s32[8,1,2]{0,2,1:T(2,128)}, u32[]{:S(2)}) copy-start(s32[8,1,2]{0,2,1:T(2,128)} %param.10) | copy-start | bytes 196
  6.0 9.5 %copy-start.2 = (bf16[768,1024]{1,0:T(8,128)(2,1)S(1)}, bf16[768,1024]{1,0:T(8,128)(2,1)}, u32[]{:S(2)}) copy-start(bf16[768,1024]{1,0:T(8,128)(2,1)} %q_ref.1) | copy-start | bytes 4718596
  6.0 48.0 %all-to-all-start = ((bf16[32,64,768]{2,1,0:T(8,128)(2,1)}), bf16[32,64,768]{2,1,0:T(8,128)(2,1)}, u32[]{:S(2)}, u32[]{:S(2)}) async-start(bf16[32,64,768]{2,1,0:T(8,128)(2,1)} %prep.1.lab_ref.refs_2_), calls=%async_computation | async-start | bytes 6291456 | tf_op jit(solution)/shard_map/all_to_all | solution.py:360
  17.3 7.4 %copy-start.10 = (s32[1,32,4]{1,2,0:T(4,128)S(1)}, s32[1,32,4]{1,2,0:T(4,128)}, u32[]{:S(2)}) copy-start(s32[1,32,4]{1,2,0:T(4,128)} %param.9) | copy-start | bytes 1540
  17.3 7.5 %copy-start.11 = (s32[1,32,4]{1,2,0:T(4,128)S(1)}, s32[1,32,4]{1,2,0:T(4,128)}, u32[]{:S(2)}) copy-start(s32[1,32,4]{1,2,0:T(4,128)} %param.8) | copy-start | bytes 1540
  17.3 21.6 %copy-start.9 = (s32[768,4]{0,1:T(4,128)S(1)}, s32[768,4]{0,1:T(4,128)}, u32[]{:S(2)}) copy-start(s32[768,4]{0,1:T(4,128)} %param.11) | copy-start | bytes 36868
  17.3 16.7 %collective-permute-start.1 = (bf16[256,1024]{1,0:T(8,128)(2,1)S(1)}, bf16[256,1024]{1,0:T(8,128)(2,1)}, u32[]{:S(2)}, u32[]{:S(2)}) collective-permute-start(bf16[256,1024]{1,0:T(8,128)(2,1)S(1)} %pack_cross.3), channel_id=1, source_target_pairs={{32,0},{64,32},{96,64},{128,96},{160,128},{192,160},{224,192},{0,2... | collective-permute-start | bytes 1572872 | tf_op jit(solution)/shard_map/ppermute | solution.py:380
  24.6 14.3 %collective-permute-start = (bf16[256,1024]{1,0:T(8,128)(2,1)S(1)}, bf16[256,1024]{1,0:T(8,128)(2,1)}, u32[]{:S(2)}, u32[]{:S(2)}) collective-permute-start(bf16[256,1024]{1,0:T(8,128)(2,1)S(1)} %pack_cross.2), channel_id=1, source_target_pairs={{0,32},{32,64},{64,96},{96,128},{128,160},{160,192},{192,224},{224... | collective-permute-start | bytes 1572872 | tf_op jit(solution)/shard_map/ppermute | solution.py:379
  47.2 1.7 %copy-start.3 = (f32[1024,768]{1,0:T(8,128)}, f32[1024,768]{1,0:T(8,128)S(1)}, u32[]{:S(2)}) copy-start(f32[1024,768]{1,0:T(8,128)S(1)} %get-tuple-element.12.mix_ref) | copy-start | bytes 9437188
  48.9 1.1 copy-start.5
  54.0 37.0 %copy-start.4 = (f32[1024,768]{1,0:T(8,128)S(1)}, f32[1024,768]{1,0:T(8,128)}, u32[]{:S(2)}) copy-start(f32[1024,768]{1,0:T(8,128)} %copy-done.3) | copy-start | bytes 9437188
  56.8 34.3 %copy-start = (f32[768,1000]{0,1:T(8,128)S(1)}, f32[768,1000]{0,1:T(8,128)}, u32[]{:S(2)}) copy-start(f32[768,1000]{0,1:T(8,128)} %param.7) | copy-start | bytes 9216004
  97.6 0.9 copy-start.7
  98.4 27.0 %all-to-all-start.2 = ((bf16[32,32,768]{2,1,0:T(8,128)(2,1)}), bf16[32,32,768]{2,1,0:T(8,128)(2,1)}, u32[]{:S(2)}, u32[]{:S(2)}) async-start(bf16[32,32,768]{2,1,0:T(8,128)(2,1)} %bitcast.6), calls=%async_computation.2 | async-start | bytes 3145728 | tf_op jit(solution)/shard_map/all_to_all | solution.py:360
  103.1 17.5 %copy-start.6 = (bf16[1024,768]{1,0:T(8,128)(2,1)S(1)}, bf16[1024,768]{1,0:T(8,128)(2,1)}, u32[]{:S(2)}) copy-start(bf16[1024,768]{1,0:T(8,128)(2,1)} %copy-done.5) | copy-start | bytes 4718596
  106.5 10.9 %collective-permute-start.3 = (bf16[1024,128]{1,0:T(8,128)(2,1)S(1)}, bf16[1024,128]{1,0:T(8,128)(2,1)S(1)}, u32[]{:S(2)}, u32[]{:S(2)}) collective-permute-start(bf16[1024,128]{1,0:T(8,128)(2,1)S(1)} %pack_labels.3), channel_id=1, source_target_pairs={{32,0},{64,32},{96,64},{128,96},{160,128},{192,160},{224,192},{0,2... | collective-permute-start | bytes 786440 | tf_op jit(solution)/shard_map/ppermute | solution.py:387
  112.1 8.5 %collective-permute-start.2 = (bf16[1024,128]{1,0:T(8,128)(2,1)S(1)}, bf16[1024,128]{1,0:T(8,128)(2,1)S(1)}, u32[]{:S(2)}, u32[]{:S(2)}) collective-permute-start(bf16[1024,128]{1,0:T(8,128)(2,1)S(1)} %pack_labels.2), channel_id=1, source_target_pairs={{0,32},{32,64},{64,96},{96,128},{128,160},{160,192},{192,224},{224... | collective-permute-start | bytes 786440 | tf_op jit(solution)/shard_map/ppermute | solution.py:386
  125.4 26.7 %copy-start.1 = (f32[768,1000]{0,1:T(8,128)S(1)}, f32[768,1000]{0,1:T(8,128)}, u32[]{:S(2)}) copy-start(f32[768,1000]{0,1:T(8,128)} %param.7) | copy-start | bytes 9216004
  125.4 26.7 %copy-start.8 = (bf16[512,768]{1,0:T(8,128)(2,1)S(1)}, bf16[512,768]{1,0:T(8,128)(2,1)}, u32[]{:S(2)}) copy-start(bf16[512,768]{1,0:T(8,128)(2,1)} %copy-done.7) | copy-start | bytes 2359300

commit v2 on v1

--- a/solution.py
+++ b/solution.py
@@ -9,6 +9,8 @@
 MIXING = 0.8
 SUB = 32
 QB = 256
+PARTS = 5
+STORES = 4
 BF = jnp.bfloat16
 F32 = jnp.float32
 VMEM_BYTES = 24 * 1024 * 1024
@@ -24,6 +26,10 @@
     return pltpu.with_memory_space_constraint(x, pltpu.HBM)
 
 
+def in_vmem(x):
+    return pltpu.with_memory_space_constraint(x, pltpu.VMEM)
+
+
 def cost(flops, size, exps=0):
     return pl.CostEstimate(flops=flops, bytes_accessed=size, transcendentals=exps)
 
@@ -37,37 +43,77 @@
 
 
 def padded(x, rows):
+    if x.shape[0] == rows:
+        return x
     return jnp.concatenate([x, jnp.zeros((rows - x.shape[0], x.shape[1]), x.dtype)], axis=0)
 
 
-def share_of(prior_ref):
-    prior = prior_ref[...]
-    return prior / jnp.sum(prior, axis=0, keepdims=True)
-
-
-def prep_kernel(prior_ref, emb_ref, out_ref):
-    relays = out_ref.shape[0]
-    labels = padded(share_of(prior_ref), relays * SUB).astype(BF)
-    out_ref[:, :SUB, :] = labels.reshape(relays, SUB, BR)
-    wide = emb_ref.shape[1] // BR
-    for r in range(BR // SUB):
-        for f in range(wide):
-            out_ref[r * wide + f, SUB:, :] = emb_ref[r * SUB : (r + 1) * SUB, f * BR : (f + 1) * BR]
+def prep_kernel(prior_ref, emb_ref, out_ref, prior_buf, emb_buf, out_buf, sem_p, sem_e, sem_o):
+    relays, _, rows = out_ref.shape
+    classes, features = prior_ref.shape[0], emb_ref.shape[1]
+    wide, tall = features // BR, BR // SUB
+    part = classes // PARTS
+    loads = [
+        pltpu.make_async_copy(
+            prior_ref.at[pl.ds(i * part, part)], prior_buf.at[pl.ds(i * part, part)], sem_p.at[i]
+        )
+        for i in range(PARTS)
+    ]
+    pieces = [
+        pltpu.make_async_copy(emb_ref.at[pl.ds(b * BR, BR)], emb_buf.at[pl.ds(b * BR, BR)], sem_e.at[b])
+        for b in range(rows // BR)
+    ]
+    for copy in (*pieces, *loads):
+        copy.start()
+    for b, copy in enumerate(pieces):
+        copy.wait()
+        for r in range(tall):
+            at = b * BR + r * SUB
+            for f in range(wide):
+                out_buf[r * wide + f, SUB:, b * BR : (b + 1) * BR] = emb_buf[
+                    at : at + SUB, f * BR : (f + 1) * BR
+                ]
+    total = jnp.zeros((8, rows), F32)
+    for i, copy in enumerate(loads):
+        copy.wait()
+        rest = prior_buf[i * part : (i + 1) * part].reshape(part // 8, 8, rows)
+        total = total + jnp.sum(rest, axis=0)
+    inverse = 1.0 / jnp.sum(total, axis=0, keepdims=True)
+    batch = relays // STORES
+    stores = []
+    for i in range(STORES):
+        for m in range(i * batch, (i + 1) * batch):
+            end = min(classes, (m + 1) * SUB)
+            share = padded(prior_buf[m * SUB : end] * inverse, SUB)
+            out_buf[m, :SUB, :] = share.astype(BF)
+        stores.append(
+            pltpu.make_async_copy(
+                out_buf.at[pl.ds(i * batch, batch)], out_ref.at[pl.ds(i * batch, batch)], sem_o.at[i]
+            )
+        )
+        stores[-1].start()
+    for copy in stores:
+        copy.wait()
 
 
 def prep(prior_t, emb, relays):
     classes, rows = prior_t.shape
     features = emb.shape[1]
+    shape = (relays, 2 * SUB, rows)
     return pl.pallas_call(
         prep_kernel,
-        grid=(rows // BR,),
-        in_specs=[
-            pl.BlockSpec((classes, BR), lambda i: (0, i)),
-            pl.BlockSpec((BR, features), lambda i: (i, 0)),
-        ],
-        out_specs=pl.BlockSpec((relays, 2 * SUB, BR), lambda i: (0, 0, i)),
-        out_shape=jax.ShapeDtypeStruct((relays, 2 * SUB, rows), BF),
-        compiler_params=params(),
+        in_specs=[pl.BlockSpec(memory_space=pl.ANY)] * 2,
+        out_specs=pl.BlockSpec(memory_space=pl.ANY),
+        out_shape=jax.ShapeDtypeStruct(shape, BF),
+        scratch_shapes=[
+            pltpu.VMEM((classes, rows), F32),
+            pltpu.VMEM((rows, features), BF),
+            pltpu.VMEM(shape, BF),
+            pltpu.SemaphoreType.DMA((PARTS,)),
+            pltpu.SemaphoreType.DMA((rows // BR,)),
+            pltpu.SemaphoreType.DMA((STORES,)),
+        ],
+        compiler_params=pltpu.CompilerParams(vmem_limit_bytes=VMEM_BYTES),
         cost_estimate=cost(4 * classes * rows, 4 * classes * rows + 4 * features * rows),
         name="prep",
     )(in_hbm(prior_t), in_hbm(emb))
@@ -76,7 +122,7 @@
 def select_kernel(owner_ref, block_ref, got_ref, after_ref, out_ref):
     members, slots = owner_ref.shape
 
-    @pl.loop(0, members)
+    @pl.loop(0, members, unroll=8)
     def _(d):
         for k in range(slots):
             lane = pl.multiple_of(block_ref[d, k] * BR, BR)
@@ -99,7 +145,7 @@
         compiler_params=pltpu.CompilerParams(vmem_limit_bytes=VMEM_BYTES),
         cost_estimate=cost(0, 4 * got.size),
         name="select",
-    )(owners, blocks, got, after)
+    )(owners, blocks, in_vmem(got), after)
 
 
 def pack_kernel(pick_ref, emb_ref, lab_ref, out_ref):
@@ -209,8 +255,8 @@
             pl.BlockSpec((8, QB), lambda i: (0, i)),
         ],
         out_shape=[
-            jax.ShapeDtypeStruct((keys, rows), BF),
-            jax.ShapeDtypeStruct((depth, rows), F32),
+            pltpu.HBM((keys, rows), BF),
+            pltpu.HBM((depth, rows), F32),
             jax.ShapeDtypeStruct((8, rows), F32),
         ],
         scratch_shapes=[pltpu.VMEM((depth, 2 * BR), BF)],
@@ -220,81 +266,85 @@
     )(emb, emb, spread, below, above, links_t)
 
 
-def near_kernel(got_ref, q_ref, links_ref, mix_ref, stat_ref, prior_ref, lab_ref, p_ref, out_ref, key_ref):
-    step = pl.program_id(0)
-    features = q_ref.shape[1]
+def near_kernel(
+    got_ref, emb_ref, links_ref, mix_ref, stat_ref, prior_ref,
+    lab_ref, p_ref, out_ref,
+    key_ref, lab_buf, p_buf, sem_l, sem_p,
+):
+    rows, features = emb_ref.shape
     relays = got_ref.shape[0]
     slots = got_ref.shape[2] // BR
     wide = features // BR
-
-    @pl.when(step == 0)
-    def _():
-        for s in range(slots):
-            for r in range(BR // SUB):
-                at = s * BR + r * SUB
-                for f in range(wide):
-                    key_ref[at : at + SUB, f * BR : (f + 1) * BR] = got_ref[
-                        r * wide + f, SUB:, s * BR : (s + 1) * BR
-                    ]
-
-    links = links_ref[...]
-    scores = nt(key_ref[...], q_ref[...]) * features ** (-0.5)
-    scores = jnp.concatenate(
-        [
-            jnp.where(slot_hit(links, s), scores[s * BR : (s + 1) * BR], -jnp.inf)
-            for s in range(slots)
-        ],
-        axis=0,
-    )
-    own_top = stat_ref[0:1]
-    top = jnp.maximum(own_top, jnp.max(scores, axis=0, keepdims=True))
-    powers = jnp.exp(scores - top)
-    lower = jnp.exp(own_top - top)
-    inverse = MIXING / (lower * stat_ref[1:2] + jnp.sum(powers, axis=0, keepdims=True))
-    lower = lower * inverse
-    powers = powers.astype(BF)
-    p_ref[...] = powers
-    out_ref[...] = jnp.concatenate([lower, inverse, jnp.zeros((6, QB), F32)], axis=0)
-    near = nn(got_ref[:, :SUB, :].reshape(relays * SUB, slots * BR), powers)
-    sharp = sharpened(mix_ref[...] * lower + near * inverse, prior_ref)
-    lab_ref[...] = padded(sharp, relays * SUB).astype(BF)
-
-
-def sharpened(mixed, prior_ref):
-    share = share_of(prior_ref)
+    for s in range(slots):
+        for r in range(BR // SUB):
+            at = s * BR + r * SUB
+            for f in range(wide):
+                key_ref[at : at + SUB, f * BR : (f + 1) * BR] = got_ref[
+                    r * wide + f, SUB:, s * BR : (s + 1) * BR
+                ]
+    near_labels = got_ref[:, :SUB, :].reshape(relays * SUB, slots * BR)
+    copies = []
+    for i in range(rows // QB):
+        at = slice(i * QB, (i + 1) * QB)
+        links = links_ref[:, at]
+        scores = nt(key_ref[...], emb_ref[at]) * features ** (-0.5)
+        scores = jnp.concatenate(
+            [
+                jnp.where(slot_hit(links, s), scores[s * BR : (s + 1) * BR], -jnp.inf)
+                for s in range(slots)
+            ],
+            axis=0,
+        )
+        own_top = stat_ref[0:1, at]
+        top = jnp.maximum(own_top, jnp.max(scores, axis=0, keepdims=True))
+        powers = jnp.exp(scores - top)
+        lower = jnp.exp(own_top - top)
+        total = lower * stat_ref[1:2, at] + jnp.sum(powers, axis=0, keepdims=True)
+        inverse = MIXING / total
+        lower = lower * inverse
+        powers = powers.astype(BF)
+        p_buf[i] = powers
+        out_ref[:, at] = jnp.concatenate([lower, inverse, jnp.zeros((6, QB), F32)], axis=0)
+        near = nn(near_labels, powers)
+        sharp = sharpened(mix_ref[:, at] * lower + near * inverse, prior_ref[:, at])
+        lab_buf[i] = padded(sharp, relays * SUB).astype(BF)
+        copies.append(pltpu.make_async_copy(lab_buf.at[i], lab_ref.at[:, pl.ds(i * QB, QB)], sem_l.at[i]))
+        copies.append(pltpu.make_async_copy(p_buf.at[i], p_ref.at[:, pl.ds(i * QB, QB)], sem_p.at[i]))
+        copies[-2].start()
+        copies[-1].start()
+    for copy in copies:
+        copy.wait()
+
+
+def sharpened(mixed, prior):
+    share = prior * (1.0 / jnp.sum(prior, axis=0, keepdims=True))
     mixed = mixed[: share.shape[0]] + (1.0 - MIXING) * share
     squared = mixed * mixed
-    return squared / jnp.sum(squared, axis=0, keepdims=True)
+    return squared * (1.0 / jnp.sum(squared, axis=0, keepdims=True))
 
 
 def near_part(got, emb, links_t, mix, stat, prior_t):
     rows, features = emb.shape
-    relays, depth2, near_keys = got.shape
-    classes = prior_t.shape[0]
-    depth = relays * SUB
+    relays, _, near_keys = got.shape
+    depth, steps = relays * SUB, rows // QB
+    whole = pl.BlockSpec(memory_space=pltpu.VMEM)
     return pl.pallas_call(
         near_kernel,
-        grid=(rows // QB,),
-        in_specs=[
-            pl.BlockSpec((relays, depth2, near_keys), lambda i: (0, 0, 0)),
-            pl.BlockSpec((QB, features), lambda i: (i, 0)),
-            pl.BlockSpec((links_t.shape[0], QB), lambda i: (0, i)),
-            pl.BlockSpec((depth, QB), lambda i: (0, i)),
-            pl.BlockSpec((8, QB), lambda i: (0, i)),
-            pl.BlockSpec((classes, QB), lambda i: (0, i)),
-        ],
-        out_specs=[
-            pl.BlockSpec((depth, QB), lambda i: (0, i)),
-            pl.BlockSpec((near_keys, QB), lambda i: (0, i)),
-            pl.BlockSpec((8, QB), lambda i: (0, i)),
-        ],
+        in_specs=[whole] * 6,
+        out_specs=[pl.BlockSpec(memory_space=pl.ANY)] * 2 + [whole],
         out_shape=[
-            jax.ShapeDtypeStruct((depth, rows), BF),
-            jax.ShapeDtypeStruct((near_keys, rows), BF),
+            pltpu.HBM((depth, rows), BF),
+            pltpu.HBM((near_keys, rows), BF),
             jax.ShapeDtypeStruct((8, rows), F32),
         ],
-        scratch_shapes=[pltpu.VMEM((near_keys, features), BF)],
-        compiler_params=params(),
+        scratch_shapes=[
+            pltpu.VMEM((near_keys, features), BF),
+            pltpu.VMEM((steps, depth, QB), BF),
+            pltpu.VMEM((steps, near_keys, QB), BF),
+            pltpu.SemaphoreType.DMA((steps,)),
+            pltpu.SemaphoreType.DMA((steps,)),
+        ],
+        compiler_params=pltpu.CompilerParams(vmem_limit_bytes=VMEM_BYTES),
         cost_estimate=cost(4 * near_keys * rows * features, 12 * depth * rows, near_keys * rows),
         name="near_part",
     )(got, emb, links_t, mix, stat, prior_t)
@@ -326,31 +376,36 @@
     )(labels_t, below, above, powers)
 
 
-def last_kernel(got_ref, p_ref, mix_ref, scale_ref, prior_ref, out_ref):
+def last_kernel(got_ref, p_ref, mix_ref, scale_ref, prior_ref, out_ref, buf, sem):
     relays, sub, near_keys = got_ref.shape
-    near = nn(got_ref[...].reshape(relays * sub, near_keys), p_ref[...])
-    mixed = mix_ref[...] * scale_ref[0:1] + near * scale_ref[1:2]
-    sharp = sharpened(mixed, prior_ref)
-    out_ref[...] = sharp * float(out_ref.shape[0])
+    classes, rows = prior_ref.shape
+    near_labels = got_ref[...].reshape(relays * sub, near_keys)
+    copies = []
+    for i in range(rows // QB):
+        at = slice(i * QB, (i + 1) * QB)
+        near = nn(near_labels, p_ref[:, at])
+        mixed = mix_ref[:, at] * scale_ref[0:1, at] + near * scale_ref[1:2, at]
+        buf[i] = sharpened(mixed, prior_ref[:, at]) * float(classes)
+        copies.append(pltpu.make_async_copy(buf.at[i], out_ref.at[:, pl.ds(i * QB, QB)], sem.at[i]))
+        copies[-1].start()
+    for copy in copies:
+        copy.wait()
 
 
 def last_part(got, powers, mix, scales, prior_t):
     relays, sub, near_keys = got.shape
     classes, rows = prior_t.shape
-    depth = relays * sub
+    depth, steps = relays * sub, rows // QB
     return pl.pallas_call(
         last_kernel,
-        grid=(rows // QB,),
-        in_specs=[
-            pl.BlockSpec((relays, sub, near_keys), lambda i: (0, 0, 0)),
-            pl.BlockSpec((near_keys, QB), lambda i: (0, i)),
-            pl.BlockSpec((depth, QB), lambda i: (0, i)),
-            pl.BlockSpec((8, QB), lambda i: (0, i)),
-            pl.BlockSpec((classes, QB), lambda i: (0, i)),
-        ],
-        out_specs=pl.BlockSpec((classes, QB), lambda i: (0, i)),
+        in_specs=[pl.BlockSpec(memory_space=pltpu.VMEM)] * 5,
+        out_specs=pl.BlockSpec(memory_space=pl.ANY),
         out_shape=jax.ShapeDtypeStruct((classes, rows), F32),
-        compiler_params=params(),
+        scratch_shapes=[
+            pltpu.VMEM((steps, classes, QB), F32),
+            pltpu.SemaphoreType.DMA((steps,)),
+        ],
+        compiler_params=pltpu.CompilerParams(vmem_limit_bytes=VMEM_BYTES),
         cost_estimate=cost(2 * near_keys * rows * depth, 12 * depth * rows),
         name="last_part",
     )(got, powers, mix, scales, prior_t)

time: 156 us -> 149 us (0.955)
  Pallas kernels: 39.6 us -> 33 us
  waiting for transfers between devices: 27.5 us -> 32.7 us
  local copies, waits for them, and re-layouts: 4.6 us -> 0.88 us
  blocking collectives: 58.9 us -> 56.3 us
    all_to_all x2, waiting for transfers between devices: 4.99 us -> 10.3 us  [exchanged(): return lax.all_to_all(x, 'member', split_axis=0, concat_axis=0, tiled=True)]
    pallas_call x3, Pallas kernels: 16 us -> 12 us  [the longest x1 4.74 us: near_part(): pl.pallas_call(near_kernel, in_specs=[whole] * 6, out_specs=[pl.BlockSpec...]
    unnamed x26 -> x24, local copies, waits for them, and re-layouts: 3.76 us -> 0.06 us
    all_to_all x2, blocking collectives: 58.9 us -> 56.3 us  [exchanged(): return lax.all_to_all(x, 'member', split_axis=0, concat_axis=0, tiled=True)]
    pallas_call x2, Pallas kernels: 3.35 us -> 1.54 us  [pack_labels(): pl.pallas_call(pack_labels_kernel, grid_spec=pltpu.PrefetchScalarGridSpec...]
  transfers between devices with their start and end apart: 6 -> 6, of which waited for: 6 -> 6; matrix products, arithmetic and copies ran while one was open for 1% -> 1% of each run, Pallas kernels for 12% -> 11%
where the time goes in v2:
time: 149 us; the launch traced here: 148 us
  blocking collectives  56.3 us (38%)
  Pallas kernels  33 us (22%)
  waiting for transfers between devices  32.7 us (22%)
  starting transfers between devices  25 us (17%)
    all_to_all x2, blocking collectives, exchanged(): return lax.all_to_all(x, 'member', split_axis=0, concat_axis=0, tiled=True)  56.3 us
    all_to_all x2, starting transfers between devices, exchanged(): return lax.all_to_all(x, 'member', split_axis=0, concat_axis=0, tiled=True)  13.6 us
    all_to_all x2, waiting for transfers between devices, exchanged(): return lax.all_to_all(x, 'member', split_axis=0, concat_axis=0, tiled=True)  10.3 us
    ppermute x1, waiting for transfers between devices, body(): above = lax.ppermute(pack(to_below, embeddings, spread), 'group', down)  9.13 us
    pallas_call x1, Pallas kernels, own_part(): pl.pallas_call(lambda *refs: own_kernel(near_slots, *refs), grid=(rows //...  9.11 us
    ppermute x1, starting transfers between devices, body(): above = lax.ppermute(pack(to_below, embeddings, spread), 'group', down)  5.65 us
    ppermute x1, starting transfers between devices, body(): above = lax.ppermute(pack_labels(to_below, labels_t), 'group', down)  5.65 us
    ppermute x1, waiting for transfers between devices, body(): above = lax.ppermute(pack_labels(to_below, labels_t), 'group', down)  5.27 us
  transfers between devices with their start and end apart: 6, of which 6 were waited for; matrix products, arithmetic and copies ran while one was open for 1% of the time, Pallas kernels for 11%

profile of v2, /device:TPU:1, one launch (start us, length us, event | category | flops | bytes accessed | tf_op | source)
XLA Modules:
  0.0 148.2 jit_solution(11752076959135382942)
XLA Ops:
  0.0 4.2 %prep.1.lab_ref.refs_2_ = bf16[32,64,768]{2,1,0:T(8,128)(2,1)} custom-call(f32[1000,768]{1,0:T(8,128)} %bitcast.8, bf16[768,1024]{1,0:T(8,128)(2,1)} %emb_ref.7), custom_call_target="tpu_custom_call" | custom-call | flops 3072000 | bytes 6217728 | tf_op jit(solution)/shard_map/prep/pallas_call | solution.py:103
  4.2 0.0 copy-start.11
  4.2 0.0 copy-start.4
  4.2 8.8 %all-to-all-start = ((bf16[32,64,768]{2,1,0:T(8,128)(2,1)}), bf16[32,64,768]{2,1,0:T(8,128)(2,1)}, u32[]{:S(2)}, u32[]{:S(2)}) async-start(bf16[32,64,768]{2,1,0:T(8,128)(2,1)} %prep.1.lab_ref.refs_2_), calls=%async_computation | async-start | bytes 6291456 | tf_op jit(solution)/shard_map/all_to_all | solution.py:415
  13.0 0.0 copy-done.11
  13.0 0.6 constant_dynamic-slice_fusion
  13.7 0.0 copy-done.4
  13.7 1.7 %pack_cross.3 = bf16[256,1024]{1,0:T(8,128)(2,1)S(1)} custom-call(s32[1]{0:T(128)} %bitcast.4.pick_ref, bf16[768,1024]{1,0:T(8,128)(2,1)S(1)} %copy-done.4, bf16[32,64,768]{2,1,0:T(8,128)(2,1)} %prep.1.lab_ref.refs_2_), custom_call_target="tpu_custom_call" | custom-call | bytes 1048576 | tf_op jit(solution)/shard_map/pack_cross/pallas_call | solution.py:161
  15.4 0.0 copy-start.9
  15.4 0.0 copy-start.10
  15.4 0.0 copy-start.8
  15.4 5.7 %collective-permute-start.1 = (bf16[256,1024]{1,0:T(8,128)(2,1)S(1)}, bf16[256,1024]{1,0:T(8,128)(2,1)}, u32[]{:S(2)}, u32[]{:S(2)}) collective-permute-start(bf16[256,1024]{1,0:T(8,128)(2,1)S(1)} %pack_cross.3), channel_id=1, source_target_pairs={{32,0},{64,32},{96,64},{128,96},{160,128},{192,160},{224,192},{0,2... | collective-permute-start | bytes 1572872 | tf_op jit(solution)/shard_map/ppermute | solution.py:435
  21.0 1.6 %pack_cross.2 = bf16[256,1024]{1,0:T(8,128)(2,1)S(1)} custom-call(s32[1]{0:T(128)} %bitcast.3.pick_ref, bf16[768,1024]{1,0:T(8,128)(2,1)S(1)} %copy-done.4, bf16[32,64,768]{2,1,0:T(8,128)(2,1)} %prep.1.lab_ref.refs_2_), custom_call_target="tpu_custom_call" | custom-call | bytes 1048576 | tf_op jit(solution)/shard_map/pack_cross/pallas_call | solution.py:161
  22.7 0.1 collective-permute-start
  22.7 0.0 copy-done.9
  22.8 0.1 copy.10.block_ref
  22.8 0.0 copy-done.10
  22.8 0.1 copy.9.owner_ref
  22.9 9.1 %collective-permute-done.1.refs_4_ = bf16[256,1024]{1,0:T(8,128)(2,1)} collective-permute-done((bf16[256,1024]{1,0:T(8,128)(2,1)S(1)}, bf16[256,1024]{1,0:T(8,128)(2,1)}, u32[]{:S(2)}, u32[]{:S(2)}) %collective-permute-start.1) | collective-permute-done | bytes 524320 | tf_op jit(solution)/shard_map/ppermute | solution.py:435
  32.1 4.9 %collective-permute-done.refs_3_ = bf16[256,1024]{1,0:T(8,128)(2,1)} collective-permute-done((bf16[256,1024]{1,0:T(8,128)(2,1)S(1)}, bf16[256,1024]{1,0:T(8,128)(2,1)}, u32[]{:S(2)}, u32[]{:S(2)}) %collective-permute-start) | collective-permute-done | bytes 524320 | tf_op jit(solution)/shard_map/ppermute | solution.py:434
  36.9 0.0 copy-done.8
  36.9 9.1 %own_part.1 = (bf16[1024,768]{1,0:T(8,128)(2,1)}, f32[1024,768]{1,0:T(8,128)}, f32[8,768]{1,0:T(8,128)S(1)}) custom-call(bf16[768,1024]{1,0:T(8,128)(2,1)S(1)} %copy-done.4, bf16[768,1024]{1,0:T(8,128)(2,1)S(1)} %copy-done.4, bf16[32,64,768]{2,1,0:T(8,128)(2,1)} %prep.1.lab_ref.refs_2_, bf16[256,1024]{1,0:T(8,128)(2,1)} %collective-permute-done.refs_3_, ...), custom_call_target="tpu_custom_call" | custom-call | flops 3221225472 | bytes 9437184 | tf_op jit(solution)/shard_map/own_part/pallas_call | solution.py:241
  46.1 6.2 %all-to-all-done.got_ref = bf16[32,64,768]{2,1,0:T(8,128)(2,1)} async-done(((bf16[32,64,768]{2,1,0:T(8,128)(2,1)}), bf16[32,64,768]{2,1,0:T(8,128)(2,1)}, u32[]{:S(2)}, u32[]{:S(2)}) %all-to-all-start) | async-done | bytes 3145760 | tf_op jit(solution)/shard_map/all_to_all | solution.py:415
  52.2 0.0 copy-start.5
  52.2 2.7 %select.6 = bf16[32,64,512]{2,1,0:T(8,128)(2,1)S(1)} custom-call(s32[32,4]{1,0:T(8,128)S(1)} %copy.9.owner_ref, s32[32,4]{1,0:T(8,128)S(1)} %copy.10.block_ref, bf16[32,64,768]{2,1,0:T(8,128)(2,1)} %all-to-all-done.got_ref, f32[8,768]{1,0:T(8,128)S(1)} %get-tuple-element.11.after_ref.stat_ref), custom_call_target="tpu_custom_call" | custom-call | bytes 6291456 | tf_op jit(solution)/shard_map/select/pallas_call | solution.py:135
  54.9 0.0 copy-start
  54.9 34.3 %all_to_all.20.got_ref = bf16[32,64,512]{2,1,0:T(8,128)(2,1)S(1)} all-to-all(bf16[32,64,512]{2,1,0:T(8,128)(2,1)S(1)} %select.6), channel_id=1, replica_groups=mesh['group'=8,'member'=32] {'member'}, dimensions={0} | all-to-all | bytes 4194304 | tf_op jit(solution)/shard_map/all_to_all | solution.py:415
  89.2 0.0 copy-done.5
  89.2 0.0 copy-done
  89.2 4.7 %near_part.1 = (bf16[1024,768]{1,0:T(8,128)(2,1)}, bf16[512,768]{1,0:T(8,128)(2,1)}, f32[8,768]{1,0:T(8,128)S(1)}) custom-call(bf16[32,64,512]{2,1,0:T(8,128)(2,1)S(1)} %all_to_all.20.got_ref, bf16[768,1024]{1,0:T(8,128)(2,1)S(1)} %copy-done.4, s32[4,768]{1,0:T(4,128)S(1)} %bitcast.13, f32[1024,768]{1,0:T(8,128)S(1)} %copy-done.5, ...), custom_call_target="tpu_custom_call" | custom-call | flops 1610612736 | bytes 9437184 | tf_op jit(solution)/shard_map/near_part/pallas_call | solution.py:331
  94.0 0.0 copy-start.2
  94.0 4.8 %all-to-all-start.2 = ((bf16[32,32,768]{2,1,0:T(8,128)(2,1)}), bf16[32,32,768]{2,1,0:T(8,128)(2,1)}, u32[]{:S(2)}, u32[]{:S(2)}) async-start(bf16[32,32,768]{2,1,0:T(8,128)(2,1)} %bitcast.11), calls=%async_computation.2 | async-start | bytes 3145728 | tf_op jit(solution)/shard_map/all_to_all | solution.py:415
  98.8 0.0 copy-done.2
  98.8 0.0 copy-start.3
  98.8 0.0 copy-start.6
  98.8 0.8 pack_labels.3
  99.7 0.7 pack_labels.2
  100.4 5.7 %collective-permute-start.3 = (bf16[1024,128]{1,0:T(8,128)(2,1)S(1)}, bf16[1024,128]{1,0:T(8,128)(2,1)S(1)}, u32[]{:S(2)}, u32[]{:S(2)}) collective-permute-start(bf16[1024,128]{1,0:T(8,128)(2,1)S(1)} %pack_labels.3), channel_id=1, source_target_pairs={{32,0},{64,32},{96,64},{128,96},{160,128},{192,160},{224,192},{0,2... | collective-permute-start | bytes 786440 | tf_op jit(solution)/shard_map/ppermute | solution.py:442
  106.0 0.0 collective-permute-start.2
  106.0 5.3 %collective-permute-done.3.above_ref = bf16[1024,128]{1,0:T(8,128)(2,1)S(1)} collective-permute-done((bf16[1024,128]{1,0:T(8,128)(2,1)S(1)}, bf16[1024,128]{1,0:T(8,128)(2,1)S(1)}, u32[]{:S(2)}, u32[]{:S(2)}) %collective-permute-start.3) | collective-permute-done | bytes 262176 | tf_op jit(solution)/shard_map/ppermute | solution.py:442
  111.3 3.2 %collective-permute-done.2.below_ref = bf16[1024,128]{1,0:T(8,128)(2,1)S(1)} collective-permute-done((bf16[1024,128]{1,0:T(8,128)(2,1)S(1)}, bf16[1024,128]{1,0:T(8,128)(2,1)S(1)}, u32[]{:S(2)}, u32[]{:S(2)}) %collective-permute-start.2) | collective-permute-done | bytes 262176 | tf_op jit(solution)/shard_map/ppermute | solution.py:441
  114.5 0.0 copy-done.3
  114.5 0.0 copy-done.6
  114.5 2.4 %remix.1.after_ref.mix_ref = f32[1024,768]{1,0:T(8,128)S(1)} custom-call(bf16[1024,768]{1,0:T(8,128)(2,1)S(1)} %copy-done.3, bf16[1024,128]{1,0:T(8,128)(2,1)S(1)} %collective-permute-done.2.below_ref, bf16[1024,128]{1,0:T(8,128)(2,1)S(1)} %collective-permute-done.3.above_ref, bf16[1024,768]{1,0:T(8,128)(2,1)S(1)} %copy-done.6), custom_call_target="tpu_custom_call" | custom-call | flops 1610612736 | bytes 6291456 | tf_op jit(solution)/shard_map/remix/pallas_call | solution.py:362
  117.0 4.1 %all-to-all-done.2.got_ref = bf16[32,32,768]{2,1,0:T(8,128)(2,1)} async-done(((bf16[32,32,768]{2,1,0:T(8,128)(2,1)}), bf16[32,32,768]{2,1,0:T(8,128)(2,1)}, u32[]{:S(2)}, u32[]{:S(2)}) %all-to-all-start.2) | async-done | bytes 1572896 | tf_op jit(solution)/shard_map/all_to_all | solution.py:415
  121.1 0.0 copy-start.1
  121.1 0.0 copy-start.7
  121.1 2.0 %select.7 = bf16[32,32,512]{2,1,0:T(8,128)(2,1)S(1)} custom-call(s32[32,4]{1,0:T(8,128)S(1)} %copy.9.owner_ref, s32[32,4]{1,0:T(8,128)S(1)} %copy.10.block_ref, bf16[32,32,768]{2,1,0:T(8,128)(2,1)} %all-to-all-done.2.got_ref, f32[1024,768]{1,0:T(8,128)S(1)} %remix.1.after_ref.mix_ref), custom_call_target="tpu_custom_call" | custom-call | bytes 3145728 | tf_op jit(solution)/shard_map/select/pallas_call | solution.py:135
  123.1 22.0 %all_to_all.21.got_ref = bf16[32,32,512]{2,1,0:T(8,128)(2,1)S(1)} all-to-all(bf16[32,32,512]{2,1,0:T(8,128)(2,1)S(1)} %select.7), channel_id=1, replica_groups=mesh['group'=8,'member'=32] {'member'}, dimensions={0} | all-to-all | bytes 2097152 | tf_op jit(solution)/shard_map/all_to_all | solution.py:415
  145.1 0.0 copy-done.1
  145.1 0.0 copy-done.7
  145.1 3.1 %last_part.1 = f32[1000,768]{1,0:T(8,128)} custom-call(bf16[32,32,512]{2,1,0:T(8,128)(2,1)S(1)} %all_to_all.21.got_ref, bf16[512,768]{1,0:T(8,128)(2,1)S(1)} %copy-done.7, f32[1024,768]{1,0:T(8,128)S(1)} %remix.1.after_ref.mix_ref, f32[8,768]{1,0:T(8,128)S(1)} %get-tuple-element.16.scale_ref, f32[1000,768]{1,0:T(8,128)S(1)} %bitcast.10), custom_call_target="tpu_custom_call" | custom-call | flops 805306368 | bytes 9437184 | tf_op jit(solution)/shard_map/last_part/pallas_call | solution.py:399
Async XLA Ops:
  4.2 8.8 %copy-start.11 = (s32[8,1,2]{0,2,1:T(2,128)S(1)}, s32[8,1,2]{0,2,1:T(2,128)}, u32[]{:S(2)}) copy-start(s32[8,1,2]{0,2,1:T(2,128)} %param.10) | copy-start | bytes 196
  4.2 9.5 %copy-start.4 = (bf16[768,1024]{1,0:T(8,128)(2,1)S(1)}, bf16[768,1024]{1,0:T(8,128)(2,1)}, u32[]{:S(2)}) copy-start(bf16[768,1024]{1,0:T(8,128)(2,1)} %emb_ref.7) | copy-start | bytes 4718596
  4.2 48.0 %all-to-all-start = ((bf16[32,64,768]{2,1,0:T(8,128)(2,1)}), bf16[32,64,768]{2,1,0:T(8,128)(2,1)}, u32[]{:S(2)}, u32[]{:S(2)}) async-start(bf16[32,64,768]{2,1,0:T(8,128)(2,1)} %prep.1.lab_ref.refs_2_), calls=%async_computation | async-start | bytes 6291456 | tf_op jit(solution)/shard_map/all_to_all | solution.py:415
  15.4 7.4 %copy-start.9 = (s32[1,32,4]{1,2,0:T(4,128)S(1)}, s32[1,32,4]{1,2,0:T(4,128)}, u32[]{:S(2)}) copy-start(s32[1,32,4]{1,2,0:T(4,128)} %param.9) | copy-start | bytes 1540
  15.4 7.5 %copy-start.10 = (s32[1,32,4]{1,2,0:T(4,128)S(1)}, s32[1,32,4]{1,2,0:T(4,128)}, u32[]{:S(2)}) copy-start(s32[1,32,4]{1,2,0:T(4,128)} %param.8) | copy-start | bytes 1540
  15.4 21.6 %copy-start.8 = (s32[768,4]{0,1:T(4,128)S(1)}, s32[768,4]{0,1:T(4,128)}, u32[]{:S(2)}) copy-start(s32[768,4]{0,1:T(4,128)} %param.11) | copy-start | bytes 36868
  15.4 16.7 %collective-permute-start.1 = (bf16[256,1024]{1,0:T(8,128)(2,1)S(1)}, bf16[256,1024]{1,0:T(8,128)(2,1)}, u32[]{:S(2)}, u32[]{:S(2)}) collective-permute-start(bf16[256,1024]{1,0:T(8,128)(2,1)S(1)} %pack_cross.3), channel_id=1, source_target_pairs={{32,0},{64,32},{96,64},{128,96},{160,128},{192,160},{224,192},{0,2... | collective-permute-start | bytes 1572872 | tf_op jit(solution)/shard_map/ppermute | solution.py:435
  22.7 14.3 %collective-permute-start = (bf16[256,1024]{1,0:T(8,128)(2,1)S(1)}, bf16[256,1024]{1,0:T(8,128)(2,1)}, u32[]{:S(2)}, u32[]{:S(2)}) collective-permute-start(bf16[256,1024]{1,0:T(8,128)(2,1)S(1)} %pack_cross.2), channel_id=1, source_target_pairs={{0,32},{32,64},{64,96},{96,128},{128,160},{160,192},{192,224},{224... | collective-permute-start | bytes 1572872 | tf_op jit(solution)/shard_map/ppermute | solution.py:434
  52.2 37.0 %copy-start.5 = (f32[1024,768]{1,0:T(8,128)S(1)}, f32[1024,768]{1,0:T(8,128)}, u32[]{:S(2)}) copy-start(f32[1024,768]{1,0:T(8,128)} %get-tuple-element.12.mix_ref) | copy-start | bytes 9437188
  54.9 34.3 %copy-start = (f32[768,1000]{0,1:T(8,128)S(1)}, f32[768,1000]{0,1:T(8,128)}, u32[]{:S(2)}) copy-start(f32[768,1000]{0,1:T(8,128)} %param.7) | copy-start | bytes 9216004
  94.0 4.8 %copy-start.2 = (bf16[1024,768]{1,0:T(8,128)(2,1)S(1)}, bf16[1024,768]{1,0:T(8,128)(2,1)}, u32[]{:S(2)}) copy-start(bf16[1024,768]{1,0:T(8,128)(2,1)} %get-tuple-element.13.lab_ref) | copy-start | bytes 4718596
  94.0 27.1 %all-to-all-start.2 = ((bf16[32,32,768]{2,1,0:T(8,128)(2,1)}), bf16[32,32,768]{2,1,0:T(8,128)(2,1)}, u32[]{:S(2)}, u32[]{:S(2)}) async-start(bf16[32,32,768]{2,1,0:T(8,128)(2,1)} %bitcast.11), calls=%async_computation.2 | async-start | bytes 3145728 | tf_op jit(solution)/shard_map/all_to_all | solution.py:415
  98.8 15.7 %copy-start.3 = (bf16[1024,768]{1,0:T(8,128)(2,1)S(1)}, bf16[1024,768]{1,0:T(8,128)(2,1)}, u32[]{:S(2)}) copy-start(bf16[1024,768]{1,0:T(8,128)(2,1)} %get-tuple-element.13.lab_ref) | copy-start | bytes 4718596
  98.8 15.7 %copy-start.6 = (bf16[1024,768]{1,0:T(8,128)(2,1)S(1)}, bf16[1024,768]{1,0:T(8,128)(2,1)}, u32[]{:S(2)}) copy-start(bf16[1024,768]{1,0:T(8,128)(2,1)} %get-tuple-element.14.p_ref) | copy-start | bytes 4718596
  100.4 10.9 %collective-permute-start.3 = (bf16[1024,128]{1,0:T(8,128)(2,1)S(1)}, bf16[1024,128]{1,0:T(8,128)(2,1)S(1)}, u32[]{:S(2)}, u32[]{:S(2)}) collective-permute-start(bf16[1024,128]{1,0:T(8,128)(2,1)S(1)} %pack_labels.3), channel_id=1, source_target_pairs={{32,0},{64,32},{96,64},{128,96},{160,128},{192,160},{224,192},{0,2... | collective-permute-start | bytes 786440 | tf_op jit(solution)/shard_map/ppermute | solution.py:442
  106.0 8.5 %collective-permute-start.2 = (bf16[1024,128]{1,0:T(8,128)(2,1)S(1)}, bf16[1024,128]{1,0:T(8,128)(2,1)S(1)}, u32[]{:S(2)}, u32[]{:S(2)}) collective-permute-start(bf16[1024,128]{1,0:T(8,128)(2,1)S(1)} %pack_labels.2), channel_id=1, source_target_pairs={{0,32},{32,64},{64,96},{96,128},{128,160},{160,192},{192,224},{224... | collective-permute-start | bytes 786440 | tf_op jit(solution)/shard_map/ppermute | solution.py:441
  121.1 24.0 %copy-start.1 = (f32[768,1000]{0,1:T(8,128)S(1)}, f32[768,1000]{0,1:T(8,128)}, u32[]{:S(2)}) copy-start(f32[768,1000]{0,1:T(8,128)} %param.7) | copy-start | bytes 9216004
  121.1 24.0 %copy-start.7 = (bf16[512,768]{1,0:T(8,128)(2,1)S(1)}, bf16[512,768]{1,0:T(8,128)(2,1)}, u32[]{:S(2)}) copy-start(bf16[512,768]{1,0:T(8,128)(2,1)} %get-tuple-element.15.p_ref) | copy-start | bytes 2359300

commit v3 on v2

--- a/solution.py
+++ b/solution.py
@@ -26,16 +26,8 @@
     return pltpu.with_memory_space_constraint(x, pltpu.HBM)
 
 
-def in_vmem(x):
-    return pltpu.with_memory_space_constraint(x, pltpu.VMEM)
-
-
 def cost(flops, size, exps=0):
     return pl.CostEstimate(flops=flops, bytes_accessed=size, transcendentals=exps)
-
-
-def nt(a, b):
-    return lax.dot_general(a, b, (((1,), (1,)), ((), ())), preferred_element_type=F32)
 
 
 def nn(a, b):
@@ -73,6 +65,12 @@
                 out_buf[r * wide + f, SUB:, b * BR : (b + 1) * BR] = emb_buf[
                     at : at + SUB, f * BR : (f + 1) * BR
                 ]
+    stores = [
+        pltpu.make_async_copy(
+            out_buf.at[:, pl.ds(SUB, SUB)], out_ref.at[:, pl.ds(SUB, SUB)], sem_o.at[STORES]
+        )
+    ]
+    stores[0].start()
     total = jnp.zeros((8, rows), F32)
     for i, copy in enumerate(loads):
         copy.wait()
@@ -80,7 +78,6 @@
         total = total + jnp.sum(rest, axis=0)
     inverse = 1.0 / jnp.sum(total, axis=0, keepdims=True)
     batch = relays // STORES
-    stores = []
     for i in range(STORES):
         for m in range(i * batch, (i + 1) * batch):
             end = min(classes, (m + 1) * SUB)
@@ -88,7 +85,9 @@
             out_buf[m, :SUB, :] = share.astype(BF)
         stores.append(
             pltpu.make_async_copy(
-                out_buf.at[pl.ds(i * batch, batch)], out_ref.at[pl.ds(i * batch, batch)], sem_o.at[i]
+                out_buf.at[pl.ds(i * batch, batch), pl.ds(0, SUB)],
+                out_ref.at[pl.ds(i * batch, batch), pl.ds(0, SUB)],
+                sem_o.at[i],
             )
         )
         stores[-1].start()
@@ -111,7 +110,7 @@
             pltpu.VMEM(shape, BF),
             pltpu.SemaphoreType.DMA((PARTS,)),
             pltpu.SemaphoreType.DMA((rows // BR,)),
-            pltpu.SemaphoreType.DMA((STORES,)),
+            pltpu.SemaphoreType.DMA((STORES + 1,)),
         ],
         compiler_params=pltpu.CompilerParams(vmem_limit_bytes=VMEM_BYTES),
         cost_estimate=cost(4 * classes * rows, 4 * classes * rows + 4 * features * rows),
@@ -145,7 +144,7 @@
         compiler_params=pltpu.CompilerParams(vmem_limit_bytes=VMEM_BYTES),
         cost_estimate=cost(0, 4 * got.size),
         name="select",
-    )(owners, blocks, in_vmem(got), after)
+    )(owners, blocks, got, after)
 
 
 def pack_kernel(pick_ref, emb_ref, lab_ref, out_ref):
@@ -173,7 +172,7 @@
         compiler_params=params(),
         cost_estimate=cost(0, 8 * BR * features),
         name="pack_cross",
-    )(pick, emb, spread)
+    )(pick, in_hbm(emb), spread)
 
 
 def pack_labels_kernel(pick_ref, lab_ref, out_ref):
@@ -201,7 +200,7 @@
     return jnp.max(jnp.where(links == slot, 1.0, 0.0), axis=0, keepdims=True) > 0.0
 
 
-def own_kernel(near_slots, emb_ref, q_ref, lab_ref, below_ref, above_ref, links_ref, p_ref, mix_ref, stat_ref, far_ref):
+def own_kernel(near_slots, emb_ref, q_ref, lab_ref, below_ref, above_ref, links_ref, prior_ref, p_ref, mix_ref, stat_ref, turned_ref, far_ref):
     step = pl.program_id(0)
     rows, features = emb_ref.shape
     depth = mix_ref.shape[0]
@@ -212,16 +211,17 @@
             for s, ref in enumerate((below_ref, above_ref)):
                 far_ref[f * BR : (f + 1) * BR, s * BR : (s + 1) * BR] = ref[BR:, f * BR : (f + 1) * BR]
 
-    q = q_ref[...]
+    q = q_ref[...].T
+    turned_ref[...] = q
     scale = features ** (-0.5)
-    own = nt(emb_ref[...], q) * scale
+    own = nn(emb_ref[...], q) * scale
     key_id = lax.broadcasted_iota(jnp.int32, own.shape, 0)
     row_id = lax.broadcasted_iota(jnp.int32, own.shape, 1) + step * QB
     own = jnp.where(key_id == row_id, -jnp.inf, own)
     links = links_ref[...]
     parts = [own]
     for s, ref in enumerate((below_ref, above_ref)):
-        far = nt(ref[:BR], q) * scale
+        far = nn(ref[:BR], q) * scale
         parts.append(jnp.where(slot_hit(links, near_slots + s), far, -jnp.inf))
     scores = jnp.concatenate(parts, axis=0)
     top = jnp.max(scores, axis=0, keepdims=True)
@@ -230,10 +230,11 @@
     powers = powers.astype(BF)
     p_ref[...] = powers
     mix_ref[...] = nn(lab_ref[...].reshape(depth, rows), powers[:rows]) + nn(far_ref[...], powers[rows:])
-    stat_ref[...] = jnp.concatenate([top, total, jnp.zeros((6, QB), F32)], axis=0)
-
-
-def own_part(emb, spread, below, above, links_t, near_slots):
+    share = (1.0 - MIXING) / jnp.sum(prior_ref[...], axis=0, keepdims=True)
+    stat_ref[...] = jnp.concatenate([top, total, share, jnp.zeros((5, QB), F32)], axis=0)
+
+
+def own_part(emb, spread, below, above, links_t, prior_t, near_slots):
     rows, features = emb.shape
     relays = spread.shape[0]
     depth = relays * SUB
@@ -248,30 +249,33 @@
             pl.BlockSpec((2 * BR, features), lambda i: (0, 0)),
             pl.BlockSpec((2 * BR, features), lambda i: (0, 0)),
             pl.BlockSpec((links_t.shape[0], QB), lambda i: (0, i)),
+            pl.BlockSpec((prior_t.shape[0], QB), lambda i: (0, i)),
         ],
         out_specs=[
             pl.BlockSpec((keys, QB), lambda i: (0, i)),
             pl.BlockSpec((depth, QB), lambda i: (0, i)),
             pl.BlockSpec((8, QB), lambda i: (0, i)),
+            pl.BlockSpec((features, QB), lambda i: (0, i)),
         ],
         out_shape=[
             pltpu.HBM((keys, rows), BF),
             pltpu.HBM((depth, rows), F32),
             jax.ShapeDtypeStruct((8, rows), F32),
+            pltpu.HBM((features, rows), BF),
         ],
         scratch_shapes=[pltpu.VMEM((depth, 2 * BR), BF)],
         compiler_params=params(),
         cost_estimate=cost(4 * keys * rows * features, 12 * depth * rows, keys * rows),
         name="own_part",
-    )(emb, emb, spread, below, above, links_t)
+    )(in_hbm(emb), in_hbm(emb), spread, below, above, links_t, in_hbm(prior_t))
 
 
 def near_kernel(
-    got_ref, emb_ref, links_ref, mix_ref, stat_ref, prior_ref,
+    got_ref, turned_ref, links_ref, mix_ref, stat_ref, prior_ref,
     lab_ref, p_ref, out_ref,
-    key_ref, lab_buf, p_buf, sem_l, sem_p,
+    key_ref, mixed_buf, lab_buf, p_buf, sem_l, sem_p,
 ):
-    rows, features = emb_ref.shape
+    features, rows = turned_ref.shape
     relays = got_ref.shape[0]
     slots = got_ref.shape[2] // BR
     wide = features // BR
@@ -287,7 +291,7 @@
     for i in range(rows // QB):
         at = slice(i * QB, (i + 1) * QB)
         links = links_ref[:, at]
-        scores = nt(key_ref[...], emb_ref[at]) * features ** (-0.5)
+        scores = nn(key_ref[...], turned_ref[:, at]) * features ** (-0.5)
         scores = jnp.concatenate(
             [
                 jnp.where(slot_hit(links, s), scores[s * BR : (s + 1) * BR], -jnp.inf)
@@ -304,10 +308,13 @@
         lower = lower * inverse
         powers = powers.astype(BF)
         p_buf[i] = powers
-        out_ref[:, at] = jnp.concatenate([lower, inverse, jnp.zeros((6, QB), F32)], axis=0)
-        near = nn(near_labels, powers)
-        sharp = sharpened(mix_ref[:, at] * lower + near * inverse, prior_ref[:, at])
-        lab_buf[i] = padded(sharp, relays * SUB).astype(BF)
+        share = stat_ref[2:3, at]
+        out_ref[:, at] = jnp.concatenate([lower, inverse, share, jnp.zeros((5, QB), F32)], axis=0)
+        mixed_buf[i] = nn(near_labels, powers)
+        norm = squares(mixed_buf.at[i], mix_ref, prior_ref, at, lower, inverse, share)
+        for start, end in tiles(prior_ref.shape[0]):
+            sharp = padded(mixed_buf[i, start:end] * norm, BR)
+            lab_buf[i, start : start + BR] = sharp.astype(BF)
         copies.append(pltpu.make_async_copy(lab_buf.at[i], lab_ref.at[:, pl.ds(i * QB, QB)], sem_l.at[i]))
         copies.append(pltpu.make_async_copy(p_buf.at[i], p_ref.at[:, pl.ds(i * QB, QB)], sem_p.at[i]))
         copies[-2].start()
@@ -316,15 +323,22 @@
         copy.wait()
 
 
-def sharpened(mixed, prior):
-    share = prior * (1.0 / jnp.sum(prior, axis=0, keepdims=True))
-    mixed = mixed[: share.shape[0]] + (1.0 - MIXING) * share
-    squared = mixed * mixed
-    return squared * (1.0 / jnp.sum(squared, axis=0, keepdims=True))
-
-
-def near_part(got, emb, links_t, mix, stat, prior_t):
-    rows, features = emb.shape
+def tiles(classes):
+    return [(start, min(start + BR, classes)) for start in range(0, classes, BR)]
+
+
+def squares(buf, mix_ref, prior_ref, at, lower, inverse, share):
+    total = jnp.zeros((8, QB), F32)
+    for start, end in tiles(prior_ref.shape[0]):
+        mixed = mix_ref[start:end, at] * lower + buf[start:end] * inverse + prior_ref[start:end, at] * share
+        mixed = mixed * mixed
+        buf[start:end] = mixed
+        total = total + jnp.sum(mixed.reshape(-1, 8, QB), axis=0)
+    return 1.0 / jnp.sum(total, axis=0, keepdims=True)
+
+
+def near_part(got, turned, links_t, mix, stat, prior_t):
+    features, rows = turned.shape
     relays, _, near_keys = got.shape
     depth, steps = relays * SUB, rows // QB
     whole = pl.BlockSpec(memory_space=pltpu.VMEM)
@@ -339,6 +353,7 @@
         ],
         scratch_shapes=[
             pltpu.VMEM((near_keys, features), BF),
+            pltpu.VMEM((steps, depth, QB), F32),
             pltpu.VMEM((steps, depth, QB), BF),
             pltpu.VMEM((steps, near_keys, QB), BF),
             pltpu.SemaphoreType.DMA((steps,)),
@@ -347,7 +362,7 @@
         compiler_params=pltpu.CompilerParams(vmem_limit_bytes=VMEM_BYTES),
         cost_estimate=cost(4 * near_keys * rows * features, 12 * depth * rows, near_keys * rows),
         name="near_part",
-    )(got, emb, links_t, mix, stat, prior_t)
+    )(got, turned, links_t, mix, stat, prior_t)
 
 
 def remix_kernel(lab_ref, below_ref, above_ref, p_ref, out_ref):
@@ -376,16 +391,18 @@
     )(labels_t, below, above, powers)
 
 
-def last_kernel(got_ref, p_ref, mix_ref, scale_ref, prior_ref, out_ref, buf, sem):
+def last_kernel(got_ref, p_ref, mix_ref, scale_ref, prior_ref, out_ref, mixed_buf, buf, sem):
     relays, sub, near_keys = got_ref.shape
     classes, rows = prior_ref.shape
     near_labels = got_ref[...].reshape(relays * sub, near_keys)
     copies = []
     for i in range(rows // QB):
         at = slice(i * QB, (i + 1) * QB)
-        near = nn(near_labels, p_ref[:, at])
-        mixed = mix_ref[:, at] * scale_ref[0:1, at] + near * scale_ref[1:2, at]
-        buf[i] = sharpened(mixed, prior_ref[:, at]) * float(classes)
+        mixed_buf[i] = nn(near_labels, p_ref[:, at])
+        scales = [scale_ref[k : k + 1, at] for k in range(3)]
+        norm = squares(mixed_buf.at[i], mix_ref, prior_ref, at, *scales) * float(classes)
+        for start, end in tiles(classes):
+            buf[i, start:end] = mixed_buf[i, start:end] * norm
         copies.append(pltpu.make_async_copy(buf.at[i], out_ref.at[:, pl.ds(i * QB, QB)], sem.at[i]))
         copies[-1].start()
     for copy in copies:
@@ -402,6 +419,7 @@
         out_specs=pl.BlockSpec(memory_space=pl.ANY),
         out_shape=jax.ShapeDtypeStruct((classes, rows), F32),
         scratch_shapes=[
+            pltpu.VMEM((steps, depth, QB), F32),
             pltpu.VMEM((steps, classes, QB), F32),
             pltpu.SemaphoreType.DMA((steps,)),
         ],
@@ -433,9 +451,9 @@
     relayed = exchanged(spread)
     below = lax.ppermute(pack(to_above, embeddings, spread), "group", up)
     above = lax.ppermute(pack(to_below, embeddings, spread), "group", down)
-    far_powers, mix, stat = own_part(embeddings, spread, below, above, links_t, near_slots)
+    far_powers, mix, stat, turned = own_part(embeddings, spread, below, above, links_t, prior_t, near_slots)
     near = exchanged(select(owners, blocks, relayed, stat))
-    labels_t, near_powers, scales = near_part(near, embeddings, links_t, mix, stat, prior_t)
+    labels_t, near_powers, scales = near_part(near, turned, links_t, mix, stat, prior_t)
 
     relayed = exchanged(labels_t.reshape(relays, SUB, rows))
     below = lax.ppermute(pack_labels(to_above, labels_t), "group", up)

time: 149 us -> 147 us (0.987)
  waiting for transfers between devices: 32.7 us -> 29.4 us
  Pallas kernels: 33 us -> 34.7 us
    all_to_all x2, waiting for transfers between devices: 10.3 us -> 6.6 us  [exchanged(): return lax.all_to_all(x, 'member', split_axis=0, concat_axis=0, tiled=True)]
    pallas_call x2, Pallas kernels: 3.27 us -> 5.17 us  [pack(): pl.pallas_call(pack_kernel, grid_spec=pltpu.PrefetchScalarGridSpec(num_sc...]
    pallas_call x1, Pallas kernels: 9.11 us -> 10.8 us  [own_part(): pl.pallas_call(lambda *refs: own_kernel(near_slots, *refs), grid=(rows //...]
  transfers between devices with their start and end apart: 6 -> 6, of which waited for: 6 -> 6; matrix products, arithmetic and copies ran while one was open for 1% -> 1% of each run, Pallas kernels for 11% -> 14%
where the time goes in v3:
time: 147 us; the launch traced here: 146 us
  blocking collectives  56.6 us (39%)
  Pallas kernels  34.7 us (24%)
  waiting for transfers between devices  29.4 us (20%)
  starting transfers between devices  24.5 us (17%)
    all_to_all x2, blocking collectives, exchanged(): return lax.all_to_all(x, 'member', split_axis=0, concat_axis=0, tiled=True)  56.6 us
    all_to_all x2, starting transfers between devices, exchanged(): return lax.all_to_all(x, 'member', split_axis=0, concat_axis=0, tiled=True)  13.4 us
    pallas_call x1, Pallas kernels, own_part(): pl.pallas_call(lambda *refs: own_kernel(near_slots, *refs), grid=(rows //...  10.8 us
    ppermute x1, waiting for transfers between devices, body(): above = lax.ppermute(pack(to_below, embeddings, spread), 'group', down)  8.58 us
    all_to_all x2, waiting for transfers between devices, exchanged(): return lax.all_to_all(x, 'member', split_axis=0, concat_axis=0, tiled=True)  6.6 us
    ppermute x1, waiting for transfers between devices, body(): below = lax.ppermute(pack(to_above, embeddings, spread), 'group', up)  5.74 us
    ppermute x1, starting transfers between devices, body(): above = lax.ppermute(pack(to_below, embeddings, spread), 'group', down)  5.58 us
    ppermute x1, starting transfers between devices, body(): above = lax.ppermute(pack_labels(to_below, labels_t), 'group', down)  5.47 us
  transfers between devices with their start and end apart: 6, of which 6 were waited for; matrix products, arithmetic and copies ran while one was open for 1% of the time, Pallas kernels for 14%

profile of v3, /device:TPU:1, one launch (start us, length us, event | category | flops | bytes accessed | tf_op | source)
XLA Modules:
  0.0 146.3 jit_solution(13886287629767607235)
XLA Ops:
  0.0 3.9 %prep.1.lab_ref.refs_2_ = bf16[32,64,768]{2,1,0:T(8,128)(2,1)} custom-call(f32[1000,768]{1,0:T(8,128)} %bitcast.8, bf16[768,1024]{1,0:T(8,128)(2,1)} %refs_1_.1), custom_call_target="tpu_custom_call" | custom-call | flops 3072000 | bytes 6217728 | tf_op jit(solution)/shard_map/prep/pallas_call | solution.py:102
  3.9 0.0 copy-start.11
  3.9 8.6 %all-to-all-start = ((bf16[32,64,768]{2,1,0:T(8,128)(2,1)}), bf16[32,64,768]{2,1,0:T(8,128)(2,1)S(1)}, u32[]{:S(2)}, u32[]{:S(2)}) async-start(bf16[32,64,768]{2,1,0:T(8,128)(2,1)} %prep.1.lab_ref.refs_2_), calls=%async_computation | async-start | bytes 6291456 | tf_op jit(solution)/shard_map/all_to_all | solution.py:433
  12.6 0.0 copy-done.11
  12.6 0.7 constant_dynamic-slice_fusion
  13.2 2.5 %pack_cross.3 = bf16[256,1024]{1,0:T(8,128)(2,1)} custom-call(s32[1]{0:T(128)} %bitcast.4.pick_ref, bf16[768,1024]{1,0:T(8,128)(2,1)} %refs_1_.1, bf16[32,64,768]{2,1,0:T(8,128)(2,1)} %prep.1.lab_ref.refs_2_), custom_call_target="tpu_custom_call" | custom-call | bytes 1048576 | tf_op jit(solution)/shard_map/pack_cross/pallas_call | solution.py:160
  15.8 5.6 %collective-permute-start.1 = (bf16[256,1024]{1,0:T(8,128)(2,1)}, bf16[256,1024]{1,0:T(8,128)(2,1)}, u32[]{:S(2)}, u32[]{:S(2)}) collective-permute-start(bf16[256,1024]{1,0:T(8,128)(2,1)} %pack_cross.3), channel_id=1, source_target_pairs={{32,0},{64,32},{96,64},{128,96},{160,128},{192,160},{224,192},{0,2... | collective-permute-start | bytes 1572872 | tf_op jit(solution)/shard_map/ppermute | solution.py:453
  21.3 0.0 copy-start.9
  21.3 0.0 copy-start.10
  21.3 0.0 copy-start.8
  21.3 2.6 %pack_cross.2 = bf16[256,1024]{1,0:T(8,128)(2,1)} custom-call(s32[1]{0:T(128)} %bitcast.3.pick_ref, bf16[768,1024]{1,0:T(8,128)(2,1)} %refs_1_.1, bf16[32,64,768]{2,1,0:T(8,128)(2,1)} %prep.1.lab_ref.refs_2_), custom_call_target="tpu_custom_call" | custom-call | bytes 1048576 | tf_op jit(solution)/shard_map/pack_cross/pallas_call | solution.py:160
  24.0 0.0 collective-permute-start
  24.0 0.0 copy-done.9
  24.0 0.1 copy.10.block_ref
  24.1 0.0 copy-done.10
  24.1 0.1 copy.9.owner_ref
  24.2 8.6 %collective-permute-done.1.refs_4_ = bf16[256,1024]{1,0:T(8,128)(2,1)} collective-permute-done((bf16[256,1024]{1,0:T(8,128)(2,1)}, bf16[256,1024]{1,0:T(8,128)(2,1)}, u32[]{:S(2)}, u32[]{:S(2)}) %collective-permute-start.1) | collective-permute-done | bytes 524320 | tf_op jit(solution)/shard_map/ppermute | solution.py:453
  32.7 5.7 %collective-permute-done.refs_3_ = bf16[256,1024]{1,0:T(8,128)(2,1)} collective-permute-done((bf16[256,1024]{1,0:T(8,128)(2,1)}, bf16[256,1024]{1,0:T(8,128)(2,1)}, u32[]{:S(2)}, u32[]{:S(2)}) %collective-permute-start) | collective-permute-done | bytes 524320 | tf_op jit(solution)/shard_map/ppermute | solution.py:452
  38.5 0.0 copy-done.8
  38.5 10.8 %own_part.1 = (bf16[1024,768]{1,0:T(8,128)(2,1)}, f32[1024,768]{1,0:T(8,128)}, f32[8,768]{1,0:T(8,128)S(1)}, bf16[1024,768]{1,0:T(8,128)(2,1)}) custom-call(bf16[768,1024]{1,0:T(8,128)(2,1)} %refs_1_.1, bf16[768,1024]{1,0:T(8,128)(2,1)} %refs_1_.1, bf16[32,64,768]{2,1,0:T(8,128)(2,1)} %prep.1.lab_ref.refs_2_, ...), custom_call_target="tpu_custom_call" | custom-call | flops 3221225472 | bytes 9437184 | tf_op jit(solution)/shard_map/own_part/pallas_call | solution.py:242
  49.3 2.4 %all-to-all-done.got_ref = bf16[32,64,768]{2,1,0:T(8,128)(2,1)S(1)} async-done(((bf16[32,64,768]{2,1,0:T(8,128)(2,1)}), bf16[32,64,768]{2,1,0:T(8,128)(2,1)S(1)}, u32[]{:S(2)}, u32[]{:S(2)}) %all-to-all-start) | async-done | bytes 3145760 | tf_op jit(solution)/shard_map/all_to_all | solution.py:433
  51.7 0.0 copy-start.4
  51.7 0.0 copy-start.6
  51.7 1.7 %select.6 = bf16[32,64,512]{2,1,0:T(8,128)(2,1)S(1)} custom-call(s32[32,4]{1,0:T(8,128)S(1)} %copy.9.owner_ref, s32[32,4]{1,0:T(8,128)S(1)} %copy.10.block_ref, bf16[32,64,768]{2,1,0:T(8,128)(2,1)S(1)} %all-to-all-done.got_ref, f32[8,768]{1,0:T(8,128)S(1)} %get-tuple-element.12.after_ref.stat_ref), custom_call_target="tpu_custom_call" | custom-call | bytes 6291456 | tf_op jit(solution)/shard_map/select/pallas_call | solution.py:134
  53.4 0.0 copy-start
  53.4 34.5 %all_to_all.20.got_ref = bf16[32,64,512]{2,1,0:T(8,128)(2,1)S(1)} all-to-all(bf16[32,64,512]{2,1,0:T(8,128)(2,1)S(1)} %select.6), channel_id=1, replica_groups=mesh['group'=8,'member'=32] {'member'}, dimensions={0} | all-to-all | bytes 4194304 | tf_op jit(solution)/shard_map/all_to_all | solution.py:433
  87.9 0.0 copy-done.4
  87.9 0.0 copy-done.6
  87.9 0.0 copy-done
  87.9 4.2 %near_part.1 = (bf16[1024,768]{1,0:T(8,128)(2,1)}, bf16[512,768]{1,0:T(8,128)(2,1)}, f32[8,768]{1,0:T(8,128)S(1)}) custom-call(bf16[32,64,512]{2,1,0:T(8,128)(2,1)S(1)} %all_to_all.20.got_ref, bf16[1024,768]{1,0:T(8,128)(2,1)S(1)} %copy-done.6, s32[4,768]{1,0:T(4,128)S(1)} %bitcast.14, f32[1024,768]{1,0:T(8,128)S(1)} %copy-done.4, ...), custom_call_target="tpu_custom_call" | custom-call | flops 1610612736 | bytes 9437184 | tf_op jit(solution)/shard_map/near_part/pallas_call | solution.py:345
  92.0 0.0 copy-start.2
  92.1 4.8 %all-to-all-start.2 = ((bf16[32,32,768]{2,1,0:T(8,128)(2,1)}), bf16[32,32,768]{2,1,0:T(8,128)(2,1)}, u32[]{:S(2)}, u32[]{:S(2)}) async-start(bf16[32,32,768]{2,1,0:T(8,128)(2,1)} %bitcast.12), calls=%async_computation.2 | async-start | bytes 3145728 | tf_op jit(solution)/shard_map/all_to_all | solution.py:433
  96.9 0.0 copy-done.2
  96.9 0.0 copy-start.3
  96.9 0.0 copy-start.5
  96.9 0.8 pack_labels.3
  97.7 0.8 pack_labels.2
  98.6 5.5 %collective-permute-start.3 = (bf16[1024,128]{1,0:T(8,128)(2,1)S(1)}, bf16[1024,128]{1,0:T(8,128)(2,1)S(1)}, u32[]{:S(2)}, u32[]{:S(2)}) collective-permute-start(bf16[1024,128]{1,0:T(8,128)(2,1)S(1)} %pack_labels.3), channel_id=1, source_target_pairs={{32,0},{64,32},{96,64},{128,96},{160,128},{192,160},{224,192},{0,2... | collective-permute-start | bytes 786440 | tf_op jit(solution)/shard_map/ppermute | solution.py:460
  104.1 0.0 collective-permute-start.2
  104.1 5.3 %collective-permute-done.3.above_ref = bf16[1024,128]{1,0:T(8,128)(2,1)S(1)} collective-permute-done((bf16[1024,128]{1,0:T(8,128)(2,1)S(1)}, bf16[1024,128]{1,0:T(8,128)(2,1)S(1)}, u32[]{:S(2)}, u32[]{:S(2)}) %collective-permute-start.3) | collective-permute-done | bytes 262176 | tf_op jit(solution)/shard_map/ppermute | solution.py:460
  109.3 3.2 %collective-permute-done.2.below_ref = bf16[1024,128]{1,0:T(8,128)(2,1)S(1)} collective-permute-done((bf16[1024,128]{1,0:T(8,128)(2,1)S(1)}, bf16[1024,128]{1,0:T(8,128)(2,1)S(1)}, u32[]{:S(2)}, u32[]{:S(2)}) %collective-permute-start.2) | collective-permute-done | bytes 262176 | tf_op jit(solution)/shard_map/ppermute | solution.py:459
  112.5 0.0 copy-done.3
  112.5 0.0 copy-done.5
  112.5 2.4 %remix.1.after_ref.mix_ref = f32[1024,768]{1,0:T(8,128)S(1)} custom-call(bf16[1024,768]{1,0:T(8,128)(2,1)S(1)} %copy-done.3, bf16[1024,128]{1,0:T(8,128)(2,1)S(1)} %collective-permute-done.2.below_ref, bf16[1024,128]{1,0:T(8,128)(2,1)S(1)} %collective-permute-done.3.above_ref, bf16[1024,768]{1,0:T(8,128)(2,1)S(1)} %copy-done.5), custom_call_target="tpu_custom_call" | custom-call | flops 1610612736 | bytes 6291456 | tf_op jit(solution)/shard_map/remix/pallas_call | solution.py:377
  115.0 4.2 %all-to-all-done.2.got_ref = bf16[32,32,768]{2,1,0:T(8,128)(2,1)} async-done(((bf16[32,32,768]{2,1,0:T(8,128)(2,1)}), bf16[32,32,768]{2,1,0:T(8,128)(2,1)}, u32[]{:S(2)}, u32[]{:S(2)}) %all-to-all-start.2) | async-done | bytes 1572896 | tf_op jit(solution)/shard_map/all_to_all | solution.py:433
  119.2 0.0 copy-start.1
  119.2 2.0 %select.7 = bf16[32,32,512]{2,1,0:T(8,128)(2,1)S(1)} custom-call(s32[32,4]{1,0:T(8,128)S(1)} %copy.9.owner_ref, s32[32,4]{1,0:T(8,128)S(1)} %copy.10.block_ref, bf16[32,32,768]{2,1,0:T(8,128)(2,1)} %all-to-all-done.2.got_ref, f32[1024,768]{1,0:T(8,128)S(1)} %remix.1.after_ref.mix_ref), custom_call_target="tpu_custom_call" | custom-call | bytes 3145728 | tf_op jit(solution)/shard_map/select/pallas_call | solution.py:134
  121.2 0.0 copy-start.7
  121.2 22.1 %all_to_all.21.got_ref = bf16[32,32,512]{2,1,0:T(8,128)(2,1)S(1)} all-to-all(bf16[32,32,512]{2,1,0:T(8,128)(2,1)S(1)} %select.7), channel_id=1, replica_groups=mesh['group'=8,'member'=32] {'member'}, dimensions={0} | all-to-all | bytes 2097152 | tf_op jit(solution)/shard_map/all_to_all | solution.py:433
  143.3 0.0 copy-done.1
  143.3 0.0 copy-done.7
  143.3 2.9 %last_part.1 = f32[1000,768]{1,0:T(8,128)} custom-call(bf16[32,32,512]{2,1,0:T(8,128)(2,1)S(1)} %all_to_all.21.got_ref, bf16[512,768]{1,0:T(8,128)(2,1)S(1)} %copy-done.7, f32[1024,768]{1,0:T(8,128)S(1)} %remix.1.after_ref.mix_ref, f32[8,768]{1,0:T(8,128)S(1)} %get-tuple-element.18.scale_ref, f32[1000,768]{1,0:T(8,128)S(1)} %bitcast.11), custom_call_target="tpu_custom_call" | custom-call | flops 805306368 | bytes 9437184 | tf_op jit(solution)/shard_map/last_part/pallas_call | solution.py:416
Async XLA Ops:
  3.9 8.7 %copy-start.11 = (s32[8,1,2]{0,2,1:T(2,128)S(1)}, s32[8,1,2]{0,2,1:T(2,128)}, u32[]{:S(2)}) copy-start(s32[8,1,2]{0,2,1:T(2,128)} %param.10) | copy-start | bytes 196
  3.9 47.8 %all-to-all-start = ((bf16[32,64,768]{2,1,0:T(8,128)(2,1)}), bf16[32,64,768]{2,1,0:T(8,128)(2,1)S(1)}, u32[]{:S(2)}, u32[]{:S(2)}) async-start(bf16[32,64,768]{2,1,0:T(8,128)(2,1)} %prep.1.lab_ref.refs_2_), calls=%async_computation | async-start | bytes 6291456 | tf_op jit(solution)/shard_map/all_to_all | solution.py:433
  15.8 17.0 %collective-permute-start.1 = (bf16[256,1024]{1,0:T(8,128)(2,1)}, bf16[256,1024]{1,0:T(8,128)(2,1)}, u32[]{:S(2)}, u32[]{:S(2)}) collective-permute-start(bf16[256,1024]{1,0:T(8,128)(2,1)} %pack_cross.3), channel_id=1, source_target_pairs={{32,0},{64,32},{96,64},{128,96},{160,128},{192,160},{224,192},{0,2... | collective-permute-start | bytes 1572872 | tf_op jit(solution)/shard_map/ppermute | solution.py:453
  21.3 2.7 %copy-start.9 = (s32[1,32,4]{1,2,0:T(4,128)S(1)}, s32[1,32,4]{1,2,0:T(4,128)}, u32[]{:S(2)}) copy-start(s32[1,32,4]{1,2,0:T(4,128)} %param.9) | copy-start | bytes 1540
  21.3 2.7 %copy-start.10 = (s32[1,32,4]{1,2,0:T(4,128)S(1)}, s32[1,32,4]{1,2,0:T(4,128)}, u32[]{:S(2)}) copy-start(s32[1,32,4]{1,2,0:T(4,128)} %param.8) | copy-start | bytes 1540
  21.3 17.1 %copy-start.8 = (s32[768,4]{0,1:T(4,128)S(1)}, s32[768,4]{0,1:T(4,128)}, u32[]{:S(2)}) copy-start(s32[768,4]{0,1:T(4,128)} %param.11) | copy-start | bytes 36868
  24.0 14.5 %collective-permute-start = (bf16[256,1024]{1,0:T(8,128)(2,1)}, bf16[256,1024]{1,0:T(8,128)(2,1)}, u32[]{:S(2)}, u32[]{:S(2)}) collective-permute-start(bf16[256,1024]{1,0:T(8,128)(2,1)} %pack_cross.2), channel_id=1, source_target_pairs={{0,32},{32,64},{64,96},{96,128},{128,160},{160,192},{192,224},{224... | collective-permute-start | bytes 1572872 | tf_op jit(solution)/shard_map/ppermute | solution.py:452
  51.7 36.2 %copy-start.4 = (f32[1024,768]{1,0:T(8,128)S(1)}, f32[1024,768]{1,0:T(8,128)}, u32[]{:S(2)}) copy-start(f32[1024,768]{1,0:T(8,128)} %get-tuple-element.14.mix_ref) | copy-start | bytes 9437188
  51.7 36.2 %copy-start.6 = (bf16[1024,768]{1,0:T(8,128)(2,1)S(1)}, bf16[1024,768]{1,0:T(8,128)(2,1)}, u32[]{:S(2)}) copy-start(bf16[1024,768]{1,0:T(8,128)(2,1)} %get-tuple-element.13.turned_ref) | copy-start | bytes 4718596
  53.4 34.5 %copy-start = (f32[768,1000]{0,1:T(8,128)S(1)}, f32[768,1000]{0,1:T(8,128)}, u32[]{:S(2)}) copy-start(f32[768,1000]{0,1:T(8,128)} %param.7) | copy-start | bytes 9216004
  92.0 4.8 %copy-start.2 = (bf16[1024,768]{1,0:T(8,128)(2,1)S(1)}, bf16[1024,768]{1,0:T(8,128)(2,1)}, u32[]{:S(2)}) copy-start(bf16[1024,768]{1,0:T(8,128)(2,1)} %get-tuple-element.15.lab_ref) | copy-start | bytes 4718596
  92.1 27.1 %all-to-all-start.2 = ((bf16[32,32,768]{2,1,0:T(8,128)(2,1)}), bf16[32,32,768]{2,1,0:T(8,128)(2,1)}, u32[]{:S(2)}, u32[]{:S(2)}) async-start(bf16[32,32,768]{2,1,0:T(8,128)(2,1)} %bitcast.12), calls=%async_computation.2 | async-start | bytes 3145728 | tf_op jit(solution)/shard_map/all_to_all | solution.py:433
  96.9 15.6 %copy-start.3 = (bf16[1024,768]{1,0:T(8,128)(2,1)S(1)}, bf16[1024,768]{1,0:T(8,128)(2,1)}, u32[]{:S(2)}) copy-start(bf16[1024,768]{1,0:T(8,128)(2,1)} %get-tuple-element.15.lab_ref) | copy-start | bytes 4718596
  96.9 15.6 %copy-start.5 = (bf16[1024,768]{1,0:T(8,128)(2,1)S(1)}, bf16[1024,768]{1,0:T(8,128)(2,1)}, u32[]{:S(2)}) copy-start(bf16[1024,768]{1,0:T(8,128)(2,1)} %get-tuple-element.16.p_ref) | copy-start | bytes 4718596
  98.6 10.7 %collective-permute-start.3 = (bf16[1024,128]{1,0:T(8,128)(2,1)S(1)}, bf16[1024,128]{1,0:T(8,128)(2,1)S(1)}, u32[]{:S(2)}, u32[]{:S(2)}) collective-permute-start(bf16[1024,128]{1,0:T(8,128)(2,1)S(1)} %pack_labels.3), channel_id=1, source_target_pairs={{32,0},{64,32},{96,64},{128,96},{160,128},{192,160},{224,192},{0,2... | collective-permute-start | bytes 786440 | tf_op jit(solution)/shard_map/ppermute | solution.py:460
  104.1 8.5 %collective-permute-start.2 = (bf16[1024,128]{1,0:T(8,128)(2,1)S(1)}, bf16[1024,128]{1,0:T(8,128)(2,1)S(1)}, u32[]{:S(2)}, u32[]{:S(2)}) collective-permute-start(bf16[1024,128]{1,0:T(8,128)(2,1)S(1)} %pack_labels.2), channel_id=1, source_target_pairs={{0,32},{32,64},{64,96},{96,128},{128,160},{160,192},{192,224},{224... | collective-permute-start | bytes 786440 | tf_op jit(solution)/shard_map/ppermute | solution.py:459
  119.2 24.2 %copy-start.1 = (f32[768,1000]{0,1:T(8,128)S(1)}, f32[768,1000]{0,1:T(8,128)}, u32[]{:S(2)}) copy-start(f32[768,1000]{0,1:T(8,128)} %param.7) | copy-start | bytes 9216004
  121.2 22.2 %copy-start.7 = (bf16[512,768]{1,0:T(8,128)(2,1)S(1)}, bf16[512,768]{1,0:T(8,128)(2,1)}, u32[]{:S(2)}) copy-start(bf16[512,768]{1,0:T(8,128)(2,1)} %get-tuple-element.17.p_ref) | copy-start | bytes 2359300

commit v4 on v3

--- a/solution.py
+++ b/solution.py
@@ -11,6 +11,7 @@
 QB = 256
 PARTS = 5
 STORES = 4
+GROUP = 2
 BF = jnp.bfloat16
 F32 = jnp.float32
 VMEM_BYTES = 24 * 1024 * 1024
@@ -308,6 +309,8 @@
         lower = lower * inverse
         powers = powers.astype(BF)
         p_buf[i] = powers
+        copies.append(pltpu.make_async_copy(p_buf.at[i], p_ref.at[:, pl.ds(i * QB, QB)], sem_p.at[i]))
+        copies[-1].start()
         share = stat_ref[2:3, at]
         out_ref[:, at] = jnp.concatenate([lower, inverse, share, jnp.zeros((5, QB), F32)], axis=0)
         mixed_buf[i] = nn(near_labels, powers)
@@ -315,10 +318,16 @@
         for start, end in tiles(prior_ref.shape[0]):
             sharp = padded(mixed_buf[i, start:end] * norm, BR)
             lab_buf[i, start : start + BR] = sharp.astype(BF)
-        copies.append(pltpu.make_async_copy(lab_buf.at[i], lab_ref.at[:, pl.ds(i * QB, QB)], sem_l.at[i]))
-        copies.append(pltpu.make_async_copy(p_buf.at[i], p_ref.at[:, pl.ds(i * QB, QB)], sem_p.at[i]))
-        copies[-2].start()
-        copies[-1].start()
+            if (start // BR) % GROUP == GROUP - 1:
+                at_rows = pl.ds(start + BR - GROUP * BR, GROUP * BR)
+                copies.append(
+                    pltpu.make_async_copy(
+                        lab_buf.at[i, at_rows],
+                        lab_ref.at[at_rows, pl.ds(i * QB, QB)],
+                        sem_l.at[i, start // (GROUP * BR)],
+                    )
+                )
+                copies[-1].start()
     for copy in copies:
         copy.wait()
 
@@ -356,7 +365,7 @@
             pltpu.VMEM((steps, depth, QB), F32),
             pltpu.VMEM((steps, depth, QB), BF),
             pltpu.VMEM((steps, near_keys, QB), BF),
-            pltpu.SemaphoreType.DMA((steps,)),
+            pltpu.SemaphoreType.DMA((steps, depth // (GROUP * BR))),
             pltpu.SemaphoreType.DMA((steps,)),
         ],
         compiler_params=pltpu.CompilerParams(vmem_limit_bytes=VMEM_BYTES),
@@ -403,8 +412,15 @@
         norm = squares(mixed_buf.at[i], mix_ref, prior_ref, at, *scales) * float(classes)
         for start, end in tiles(classes):
             buf[i, start:end] = mixed_buf[i, start:end] * norm
-        copies.append(pltpu.make_async_copy(buf.at[i], out_ref.at[:, pl.ds(i * QB, QB)], sem.at[i]))
-        copies[-1].start()
+            if (start // BR) % GROUP == GROUP - 1 or end == classes:
+                first = start // (GROUP * BR)
+                at_rows = pl.ds(first * GROUP * BR, end - first * GROUP * BR)
+                copies.append(
+                    pltpu.make_async_copy(
+                        buf.at[i, at_rows], out_ref.at[at_rows, pl.ds(i * QB, QB)], sem.at[i, first]
+                    )
+                )
+                copies[-1].start()
     for copy in copies:
         copy.wait()
 
@@ -421,7 +437,7 @@
         scratch_shapes=[
             pltpu.VMEM((steps, depth, QB), F32),
             pltpu.VMEM((steps, classes, QB), F32),
-            pltpu.SemaphoreType.DMA((steps,)),
+            pltpu.SemaphoreType.DMA((steps, depth // (GROUP * BR))),
         ],
         compiler_params=pltpu.CompilerParams(vmem_limit_bytes=VMEM_BYTES),
         cost_estimate=cost(2 * near_keys * rows * depth, 12 * depth * rows),

time: 147 us -> 147 us (level)
  no operation moved by 1% of the time
where the time goes in v4:
time: 147 us; the launch traced here: 146 us
  blocking collectives  56.6 us (39%)
  Pallas kernels  34.6 us (24%)
  waiting for transfers between devices  29.4 us (20%)
  starting transfers between devices  24.5 us (17%)
    all_to_all x2, blocking collectives, exchanged(): return lax.all_to_all(x, 'member', split_axis=0, concat_axis=0, tiled=True)  56.6 us
    all_to_all x2, starting transfers between devices, exchanged(): return lax.all_to_all(x, 'member', split_axis=0, concat_axis=0, tiled=True)  13.4 us
    pallas_call x1, Pallas kernels, own_part(): pl.pallas_call(lambda *refs: own_kernel(near_slots, *refs), grid=(rows //...  10.8 us
    ppermute x1, waiting for transfers between devices, body(): above = lax.ppermute(pack(to_below, embeddings, spread), 'group', down)  8.58 us
    all_to_all x2, waiting for transfers between devices, exchanged(): return lax.all_to_all(x, 'member', split_axis=0, concat_axis=0, tiled=True)  6.59 us
    ppermute x1, waiting for transfers between devices, body(): below = lax.ppermute(pack(to_above, embeddings, spread), 'group', up)  5.74 us
    ppermute x1, starting transfers between devices, body(): above = lax.ppermute(pack(to_below, embeddings, spread), 'group', down)  5.58 us
    ppermute x1, starting transfers between devices, body(): above = lax.ppermute(pack_labels(to_below, labels_t), 'group', down)  5.47 us
  transfers between devices with their start and end apart: 6, of which 6 were waited for; matrix products, arithmetic and copies ran while one was open for 1% of the time, Pallas kernels for 14%

profile of v4, /device:TPU:1, one launch (start us, length us, event | category | flops | bytes accessed | tf_op | source)
XLA Modules:
  0.0 146.1 jit_solution(12103172178196726175)
XLA Ops:
  0.0 3.9 %prep.1.lab_ref.refs_2_ = bf16[32,64,768]{2,1,0:T(8,128)(2,1)} custom-call(f32[1000,768]{1,0:T(8,128)} %bitcast.8, bf16[768,1024]{1,0:T(8,128)(2,1)} %refs_1_.1), custom_call_target="tpu_custom_call" | custom-call | flops 3072000 | bytes 6217728 | tf_op jit(solution)/shard_map/prep/pallas_call | solution.py:103
  3.9 0.0 copy-start.11
  3.9 8.6 %all-to-all-start = ((bf16[32,64,768]{2,1,0:T(8,128)(2,1)}), bf16[32,64,768]{2,1,0:T(8,128)(2,1)S(1)}, u32[]{:S(2)}, u32[]{:S(2)}) async-start(bf16[32,64,768]{2,1,0:T(8,128)(2,1)} %prep.1.lab_ref.refs_2_), calls=%async_computation | async-start | bytes 6291456 | tf_op jit(solution)/shard_map/all_to_all | solution.py:449
  12.6 0.0 copy-done.11
  12.6 0.7 constant_dynamic-slice_fusion
  13.2 2.5 %pack_cross.3 = bf16[256,1024]{1,0:T(8,128)(2,1)} custom-call(s32[1]{0:T(128)} %bitcast.4.pick_ref, bf16[768,1024]{1,0:T(8,128)(2,1)} %refs_1_.1, bf16[32,64,768]{2,1,0:T(8,128)(2,1)} %prep.1.lab_ref.refs_2_), custom_call_target="tpu_custom_call" | custom-call | bytes 1048576 | tf_op jit(solution)/shard_map/pack_cross/pallas_call | solution.py:161
  15.8 5.6 %collective-permute-start.1 = (bf16[256,1024]{1,0:T(8,128)(2,1)}, bf16[256,1024]{1,0:T(8,128)(2,1)}, u32[]{:S(2)}, u32[]{:S(2)}) collective-permute-start(bf16[256,1024]{1,0:T(8,128)(2,1)} %pack_cross.3), channel_id=1, source_target_pairs={{32,0},{64,32},{96,64},{128,96},{160,128},{192,160},{224,192},{0,2... | collective-permute-start | bytes 1572872 | tf_op jit(solution)/shard_map/ppermute | solution.py:469
  21.3 0.0 copy-start.9
  21.3 0.0 copy-start.10
  21.3 0.0 copy-start.8
  21.3 2.6 %pack_cross.2 = bf16[256,1024]{1,0:T(8,128)(2,1)} custom-call(s32[1]{0:T(128)} %bitcast.3.pick_ref, bf16[768,1024]{1,0:T(8,128)(2,1)} %refs_1_.1, bf16[32,64,768]{2,1,0:T(8,128)(2,1)} %prep.1.lab_ref.refs_2_), custom_call_target="tpu_custom_call" | custom-call | bytes 1048576 | tf_op jit(solution)/shard_map/pack_cross/pallas_call | solution.py:161
  24.0 0.0 collective-permute-start
  24.0 0.0 copy-done.9
  24.0 0.1 copy.10.block_ref
  24.1 0.0 copy-done.10
  24.1 0.1 copy.9.owner_ref
  24.2 8.6 %collective-permute-done.1.refs_4_ = bf16[256,1024]{1,0:T(8,128)(2,1)} collective-permute-done((bf16[256,1024]{1,0:T(8,128)(2,1)}, bf16[256,1024]{1,0:T(8,128)(2,1)}, u32[]{:S(2)}, u32[]{:S(2)}) %collective-permute-start.1) | collective-permute-done | bytes 524320 | tf_op jit(solution)/shard_map/ppermute | solution.py:469
  32.7 5.7 %collective-permute-done.refs_3_ = bf16[256,1024]{1,0:T(8,128)(2,1)} collective-permute-done((bf16[256,1024]{1,0:T(8,128)(2,1)}, bf16[256,1024]{1,0:T(8,128)(2,1)}, u32[]{:S(2)}, u32[]{:S(2)}) %collective-permute-start) | collective-permute-done | bytes 524320 | tf_op jit(solution)/shard_map/ppermute | solution.py:468
  38.5 0.0 copy-done.8
  38.5 10.8 %own_part.1 = (bf16[1024,768]{1,0:T(8,128)(2,1)}, f32[1024,768]{1,0:T(8,128)}, f32[8,768]{1,0:T(8,128)S(1)}, bf16[1024,768]{1,0:T(8,128)(2,1)}) custom-call(bf16[768,1024]{1,0:T(8,128)(2,1)} %refs_1_.1, bf16[768,1024]{1,0:T(8,128)(2,1)} %refs_1_.1, bf16[32,64,768]{2,1,0:T(8,128)(2,1)} %prep.1.lab_ref.refs_2_, ...), custom_call_target="tpu_custom_call" | custom-call | flops 3221225472 | bytes 9437184 | tf_op jit(solution)/shard_map/own_part/pallas_call | solution.py:243
  49.3 2.4 %all-to-all-done.got_ref = bf16[32,64,768]{2,1,0:T(8,128)(2,1)S(1)} async-done(((bf16[32,64,768]{2,1,0:T(8,128)(2,1)}), bf16[32,64,768]{2,1,0:T(8,128)(2,1)S(1)}, u32[]{:S(2)}, u32[]{:S(2)}) %all-to-all-start) | async-done | bytes 3145760 | tf_op jit(solution)/shard_map/all_to_all | solution.py:449
  51.7 0.0 copy-start.4
  51.7 0.0 copy-start.6
  51.7 1.7 %select.6 = bf16[32,64,512]{2,1,0:T(8,128)(2,1)S(1)} custom-call(s32[32,4]{1,0:T(8,128)S(1)} %copy.9.owner_ref, s32[32,4]{1,0:T(8,128)S(1)} %copy.10.block_ref, bf16[32,64,768]{2,1,0:T(8,128)(2,1)S(1)} %all-to-all-done.got_ref, f32[8,768]{1,0:T(8,128)S(1)} %get-tuple-element.12.after_ref.stat_ref), custom_call_target="tpu_custom_call" | custom-call | bytes 6291456 | tf_op jit(solution)/shard_map/select/pallas_call | solution.py:135
  53.4 0.0 copy-start
  53.4 34.5 %all_to_all.20.got_ref = bf16[32,64,512]{2,1,0:T(8,128)(2,1)S(1)} all-to-all(bf16[32,64,512]{2,1,0:T(8,128)(2,1)S(1)} %select.6), channel_id=1, replica_groups=mesh['group'=8,'member'=32] {'member'}, dimensions={0} | all-to-all | bytes 4194304 | tf_op jit(solution)/shard_map/all_to_all | solution.py:449
  87.9 0.0 copy-done.4
  87.9 0.0 copy-done.6
  87.9 0.0 copy-done
  87.9 4.2 %near_part.1 = (bf16[1024,768]{1,0:T(8,128)(2,1)}, bf16[512,768]{1,0:T(8,128)(2,1)}, f32[8,768]{1,0:T(8,128)S(1)}) custom-call(bf16[32,64,512]{2,1,0:T(8,128)(2,1)S(1)} %all_to_all.20.got_ref, bf16[1024,768]{1,0:T(8,128)(2,1)S(1)} %copy-done.6, s32[4,768]{1,0:T(4,128)S(1)} %bitcast.14, f32[1024,768]{1,0:T(8,128)S(1)} %copy-done.4, ...), custom_call_target="tpu_custom_call" | custom-call | flops 1610612736 | bytes 9437184 | tf_op jit(solution)/shard_map/near_part/pallas_call | solution.py:354
  92.1 0.0 copy-start.2
  92.1 4.8 %all-to-all-start.2 = ((bf16[32,32,768]{2,1,0:T(8,128)(2,1)}), bf16[32,32,768]{2,1,0:T(8,128)(2,1)}, u32[]{:S(2)}, u32[]{:S(2)}) async-start(bf16[32,32,768]{2,1,0:T(8,128)(2,1)} %bitcast.12), calls=%async_computation.2 | async-start | bytes 3145728 | tf_op jit(solution)/shard_map/all_to_all | solution.py:449
  96.9 0.0 copy-done.2
  96.9 0.0 copy-start.3
  96.9 0.0 copy-start.5
  96.9 0.8 pack_labels.3
  97.8 0.8 pack_labels.2
  98.6 5.5 %collective-permute-start.3 = (bf16[1024,128]{1,0:T(8,128)(2,1)S(1)}, bf16[1024,128]{1,0:T(8,128)(2,1)S(1)}, u32[]{:S(2)}, u32[]{:S(2)}) collective-permute-start(bf16[1024,128]{1,0:T(8,128)(2,1)S(1)} %pack_labels.3), channel_id=1, source_target_pairs={{32,0},{64,32},{96,64},{128,96},{160,128},{192,160},{224,192},{0,2... | collective-permute-start | bytes 786440 | tf_op jit(solution)/shard_map/ppermute | solution.py:476
  104.1 0.0 collective-permute-start.2
  104.1 5.3 %collective-permute-done.3.above_ref = bf16[1024,128]{1,0:T(8,128)(2,1)S(1)} collective-permute-done((bf16[1024,128]{1,0:T(8,128)(2,1)S(1)}, bf16[1024,128]{1,0:T(8,128)(2,1)S(1)}, u32[]{:S(2)}, u32[]{:S(2)}) %collective-permute-start.3) | collective-permute-done | bytes 262176 | tf_op jit(solution)/shard_map/ppermute | solution.py:476
  109.3 3.2 %collective-permute-done.2.below_ref = bf16[1024,128]{1,0:T(8,128)(2,1)S(1)} collective-permute-done((bf16[1024,128]{1,0:T(8,128)(2,1)S(1)}, bf16[1024,128]{1,0:T(8,128)(2,1)S(1)}, u32[]{:S(2)}, u32[]{:S(2)}) %collective-permute-start.2) | collective-permute-done | bytes 262176 | tf_op jit(solution)/shard_map/ppermute | solution.py:475
  112.5 0.0 copy-done.3
  112.5 0.0 copy-done.5
  112.5 2.4 %remix.1.after_ref.mix_ref = f32[1024,768]{1,0:T(8,128)S(1)} custom-call(bf16[1024,768]{1,0:T(8,128)(2,1)S(1)} %copy-done.3, bf16[1024,128]{1,0:T(8,128)(2,1)S(1)} %collective-permute-done.2.below_ref, bf16[1024,128]{1,0:T(8,128)(2,1)S(1)} %collective-permute-done.3.above_ref, bf16[1024,768]{1,0:T(8,128)(2,1)S(1)} %copy-done.5), custom_call_target="tpu_custom_call" | custom-call | flops 1610612736 | bytes 6291456 | tf_op jit(solution)/shard_map/remix/pallas_call | solution.py:386
  115.0 4.2 %all-to-all-done.2.got_ref = bf16[32,32,768]{2,1,0:T(8,128)(2,1)} async-done(((bf16[32,32,768]{2,1,0:T(8,128)(2,1)}), bf16[32,32,768]{2,1,0:T(8,128)(2,1)}, u32[]{:S(2)}, u32[]{:S(2)}) %all-to-all-start.2) | async-done | bytes 1572896 | tf_op jit(solution)/shard_map/all_to_all | solution.py:449
  119.2 0.0 copy-start.1
  119.2 2.0 %select.7 = bf16[32,32,512]{2,1,0:T(8,128)(2,1)S(1)} custom-call(s32[32,4]{1,0:T(8,128)S(1)} %copy.9.owner_ref, s32[32,4]{1,0:T(8,128)S(1)} %copy.10.block_ref, bf16[32,32,768]{2,1,0:T(8,128)(2,1)} %all-to-all-done.2.got_ref, f32[1024,768]{1,0:T(8,128)S(1)} %remix.1.after_ref.mix_ref), custom_call_target="tpu_custom_call" | custom-call | bytes 3145728 | tf_op jit(solution)/shard_map/select/pallas_call | solution.py:135
  121.2 0.0 copy-start.7
  121.2 22.1 %all_to_all.21.got_ref = bf16[32,32,512]{2,1,0:T(8,128)(2,1)S(1)} all-to-all(bf16[32,32,512]{2,1,0:T(8,128)(2,1)S(1)} %select.7), channel_id=1, replica_groups=mesh['group'=8,'member'=32] {'member'}, dimensions={0} | all-to-all | bytes 2097152 | tf_op jit(solution)/shard_map/all_to_all | solution.py:449
  143.3 0.0 copy-done.1
  143.3 0.0 copy-done.7
  143.4 2.8 %last_part.1 = f32[1000,768]{1,0:T(8,128)} custom-call(bf16[32,32,512]{2,1,0:T(8,128)(2,1)S(1)} %all_to_all.21.got_ref, bf16[512,768]{1,0:T(8,128)(2,1)S(1)} %copy-done.7, f32[1024,768]{1,0:T(8,128)S(1)} %remix.1.after_ref.mix_ref, f32[8,768]{1,0:T(8,128)S(1)} %get-tuple-element.18.scale_ref, f32[1000,768]{1,0:T(8,128)S(1)} %bitcast.11), custom_call_target="tpu_custom_call" | custom-call | flops 805306368 | bytes 9437184 | tf_op jit(solution)/shard_map/last_part/pallas_call | solution.py:432
Async XLA Ops:
  3.9 8.7 %copy-start.11 = (s32[8,1,2]{0,2,1:T(2,128)S(1)}, s32[8,1,2]{0,2,1:T(2,128)}, u32[]{:S(2)}) copy-start(s32[8,1,2]{0,2,1:T(2,128)} %param.10) | copy-start | bytes 196
  3.9 47.8 %all-to-all-start = ((bf16[32,64,768]{2,1,0:T(8,128)(2,1)}), bf16[32,64,768]{2,1,0:T(8,128)(2,1)S(1)}, u32[]{:S(2)}, u32[]{:S(2)}) async-start(bf16[32,64,768]{2,1,0:T(8,128)(2,1)} %prep.1.lab_ref.refs_2_), calls=%async_computation | async-start | bytes 6291456 | tf_op jit(solution)/shard_map/all_to_all | solution.py:449
  15.8 17.0 %collective-permute-start.1 = (bf16[256,1024]{1,0:T(8,128)(2,1)}, bf16[256,1024]{1,0:T(8,128)(2,1)}, u32[]{:S(2)}, u32[]{:S(2)}) collective-permute-start(bf16[256,1024]{1,0:T(8,128)(2,1)} %pack_cross.3), channel_id=1, source_target_pairs={{32,0},{64,32},{96,64},{128,96},{160,128},{192,160},{224,192},{0,2... | collective-permute-start | bytes 1572872 | tf_op jit(solution)/shard_map/ppermute | solution.py:469
  21.3 2.7 %copy-start.9 = (s32[1,32,4]{1,2,0:T(4,128)S(1)}, s32[1,32,4]{1,2,0:T(4,128)}, u32[]{:S(2)}) copy-start(s32[1,32,4]{1,2,0:T(4,128)} %param.9) | copy-start | bytes 1540
  21.3 2.7 %copy-start.10 = (s32[1,32,4]{1,2,0:T(4,128)S(1)}, s32[1,32,4]{1,2,0:T(4,128)}, u32[]{:S(2)}) copy-start(s32[1,32,4]{1,2,0:T(4,128)} %param.8) | copy-start | bytes 1540
  21.3 17.1 %copy-start.8 = (s32[768,4]{0,1:T(4,128)S(1)}, s32[768,4]{0,1:T(4,128)}, u32[]{:S(2)}) copy-start(s32[768,4]{0,1:T(4,128)} %param.11) | copy-start | bytes 36868
  24.0 14.5 %collective-permute-start = (bf16[256,1024]{1,0:T(8,128)(2,1)}, bf16[256,1024]{1,0:T(8,128)(2,1)}, u32[]{:S(2)}, u32[]{:S(2)}) collective-permute-start(bf16[256,1024]{1,0:T(8,128)(2,1)} %pack_cross.2), channel_id=1, source_target_pairs={{0,32},{32,64},{64,96},{96,128},{128,160},{160,192},{192,224},{224... | collective-permute-start | bytes 1572872 | tf_op jit(solution)/shard_map/ppermute | solution.py:468
  51.7 36.2 %copy-start.4 = (f32[1024,768]{1,0:T(8,128)S(1)}, f32[1024,768]{1,0:T(8,128)}, u32[]{:S(2)}) copy-start(f32[1024,768]{1,0:T(8,128)} %get-tuple-element.14.mix_ref) | copy-start | bytes 9437188
  51.7 36.2 %copy-start.6 = (bf16[1024,768]{1,0:T(8,128)(2,1)S(1)}, bf16[1024,768]{1,0:T(8,128)(2,1)}, u32[]{:S(2)}) copy-start(bf16[1024,768]{1,0:T(8,128)(2,1)} %get-tuple-element.13.turned_ref) | copy-start | bytes 4718596
  53.4 34.5 %copy-start = (f32[768,1000]{0,1:T(8,128)S(1)}, f32[768,1000]{0,1:T(8,128)}, u32[]{:S(2)}) copy-start(f32[768,1000]{0,1:T(8,128)} %param.7) | copy-start | bytes 9216004
  92.1 4.8 %copy-start.2 = (bf16[1024,768]{1,0:T(8,128)(2,1)S(1)}, bf16[1024,768]{1,0:T(8,128)(2,1)}, u32[]{:S(2)}) copy-start(bf16[1024,768]{1,0:T(8,128)(2,1)} %get-tuple-element.15.lab_ref) | copy-start | bytes 4718596
  92.1 27.1 %all-to-all-start.2 = ((bf16[32,32,768]{2,1,0:T(8,128)(2,1)}), bf16[32,32,768]{2,1,0:T(8,128)(2,1)}, u32[]{:S(2)}, u32[]{:S(2)}) async-start(bf16[32,32,768]{2,1,0:T(8,128)(2,1)} %bitcast.12), calls=%async_computation.2 | async-start | bytes 3145728 | tf_op jit(solution)/shard_map/all_to_all | solution.py:449
  96.9 15.6 %copy-start.3 = (bf16[1024,768]{1,0:T(8,128)(2,1)S(1)}, bf16[1024,768]{1,0:T(8,128)(2,1)}, u32[]{:S(2)}) copy-start(bf16[1024,768]{1,0:T(8,128)(2,1)} %get-tuple-element.15.lab_ref) | copy-start | bytes 4718596
  96.9 15.6 %copy-start.5 = (bf16[1024,768]{1,0:T(8,128)(2,1)S(1)}, bf16[1024,768]{1,0:T(8,128)(2,1)}, u32[]{:S(2)}) copy-start(bf16[1024,768]{1,0:T(8,128)(2,1)} %get-tuple-element.16.p_ref) | copy-start | bytes 4718596
  98.6 10.7 %collective-permute-start.3 = (bf16[1024,128]{1,0:T(8,128)(2,1)S(1)}, bf16[1024,128]{1,0:T(8,128)(2,1)S(1)}, u32[]{:S(2)}, u32[]{:S(2)}) collective-permute-start(bf16[1024,128]{1,0:T(8,128)(2,1)S(1)} %pack_labels.3), channel_id=1, source_target_pairs={{32,0},{64,32},{96,64},{128,96},{160,128},{192,160},{224,192},{0,2... | collective-permute-start | bytes 786440 | tf_op jit(solution)/shard_map/ppermute | solution.py:476
  104.1 8.5 %collective-permute-start.2 = (bf16[1024,128]{1,0:T(8,128)(2,1)S(1)}, bf16[1024,128]{1,0:T(8,128)(2,1)S(1)}, u32[]{:S(2)}, u32[]{:S(2)}) collective-permute-start(bf16[1024,128]{1,0:T(8,128)(2,1)S(1)} %pack_labels.2), channel_id=1, source_target_pairs={{0,32},{32,64},{64,96},{96,128},{128,160},{160,192},{192,224},{224... | collective-permute-start | bytes 786440 | tf_op jit(solution)/shard_map/ppermute | solution.py:475
  119.2 24.2 %copy-start.1 = (f32[768,1000]{0,1:T(8,128)S(1)}, f32[768,1000]{0,1:T(8,128)}, u32[]{:S(2)}) copy-start(f32[768,1000]{0,1:T(8,128)} %param.7) | copy-start | bytes 9216004
  121.2 22.2 %copy-start.7 = (bf16[512,768]{1,0:T(8,128)(2,1)S(1)}, bf16[512,768]{1,0:T(8,128)(2,1)}, u32[]{:S(2)}) copy-start(bf16[512,768]{1,0:T(8,128)(2,1)} %get-tuple-element.17.p_ref) | copy-start | bytes 2359300
